TPU v7x, 256 devices: a whole 4x4x8 slice. The times are simulated.
256 devices in a mesh: dp: 16 (over z_hi, x), sp: 16 (over y, z_lo, core).
Axes of the slice: x: 4, y: 4, z: 8 (z_hi: 4, z_lo: 2; z = z_hi * 2 + z_lo), core: 2. Of those that a mesh axis runs over, the one named last changes fastest.
Arguments:
- features: bfloat16 [16, 32, 128, 640], P('dp', 'sp'), may hold values from -20 to 20
- timestep: int32 [16], P('dp'), may hold values from 0 to 999
- group_gain: float32 [640], replicated, may hold values from 0.5 to 1.5
- conv_weight: bfloat16 [3, 3, 640, 640], replicated, may hold values from -0.078125 to 0.078125
- time_weight: bfloat16 [320, 640], replicated, may hold values from -0.3125 to 0.3125
- norm_gain: float32 [640], replicated, may hold values from 0.5 to 1.5
- qkv_weight: bfloat16 [640, 1920], replicated, may hold values from -6 to 6
- out_weight: bfloat16 [640, 640], replicated, may hold values from -0.25 to 0.25
- cotangent: bfloat16 [16, 32, 128, 640], P('dp', 'sp'), may hold values from -1 to 1
Outputs:
- updated: bfloat16 [16, 32, 128, 640], P('dp', 'sp')
- out_grad: float32 [640, 640], replicated
All inputs are finite; a program needn't handle non-finite values.
Results may differ from a plain program's by a relative error of at most 0.02.
Values may be sent and summed in bfloat16 or wider, within the bound.
A program may use at most 128 MiB of HBM per device.

v0:
```python
import math

import jax
import jax.numpy as jnp
from jax import lax
from jax.sharding import PartitionSpec as P

HEADS = 16
GROUPS = 32


def with_halo(block, sides, width):
    for axis, dim in sides:
        count = lax.axis_size(axis)
        forward = [(i, i + 1) for i in range(count - 1)]
        backward = [(target, source) for source, target in forward]
        low = lax.ppermute(
            lax.slice_in_dim(block, block.shape[dim] - width, None, axis=dim), axis, forward
        )
        high = lax.ppermute(lax.slice_in_dim(block, 0, width, axis=dim), axis, backward)
        block = jnp.concatenate([low, block, high], axis=dim)
    return block


def attend_block(queries, key_rows, value_rows, score_scale):
    scores = (
        lax.dot_general(
            queries, key_rows, (((1,), (1,)), ((), ())), preferred_element_type=jnp.float32
        )
        * score_scale
    )
    row_top = jnp.max(scores, axis=-1, keepdims=True)
    weights = jnp.exp(scores - row_top)
    probabilities = (weights / jnp.sum(weights, axis=-1, keepdims=True)).astype(jnp.bfloat16)
    return jnp.dot(probabilities, value_rows, preferred_element_type=jnp.float32)


def time_embed(timestep, time_weight):
    half_dim = time_weight.shape[0] // 2
    frequencies = jnp.exp(-math.log(10000.0) * jnp.arange(half_dim, dtype=jnp.float32) / half_dim)
    angles = timestep.astype(jnp.float32)[:, None] * frequencies[None, :]
    embedding = jnp.concatenate([jnp.cos(angles), jnp.sin(angles)], axis=-1)
    embed_act = jax.nn.silu(embedding).astype(jnp.bfloat16)
    return jnp.dot(embed_act, time_weight, preferred_element_type=jnp.float32)


def layer_norm(hidden, norm_gain):
    float_hidden = hidden.astype(jnp.float32)
    centred = float_hidden - jnp.mean(float_hidden, axis=-1, keepdims=True)
    variance = jnp.mean(centred * centred, axis=-1, keepdims=True)
    return (centred * lax.rsqrt(variance + 1e-05) * norm_gain).astype(jnp.bfloat16)


def conv_taps(padded, conv_weight, row_count, grid_width):
    channels = padded.shape[-1]
    total = jnp.zeros((row_count * grid_width, channels), jnp.float32)
    for row_off in range(3):
        for col_off in range(3):
            window = padded[
                0, row_off : row_off + row_count, col_off : col_off + grid_width
            ].reshape(-1, channels)
            total = total + jnp.dot(
                window, conv_weight[row_off, col_off], preferred_element_type=jnp.float32
            )
    return total


def on_device(
    features,
    timestep,
    group_gain,
    conv_weight,
    time_weight,
    norm_gain,
    qkv_weight,
    out_weight,
    cotangent,
):
    row_count, grid_width, channels = (features.shape[1], features.shape[2], features.shape[3])
    slabs = lax.axis_size("sp")
    tokens_here = row_count * grid_width
    per_group = channels // GROUPS
    float_feats = features.astype(jnp.float32).reshape(tokens_here, GROUPS, per_group)
    total_sum, total_squares = lax.psum(
        (jnp.sum(float_feats, axis=(0, 2)), jnp.sum(float_feats * float_feats, axis=(0, 2))), "sp"
    )
    cell_count = row_count * slabs * grid_width * per_group
    group_mean = total_sum / cell_count
    group_var = total_squares / cell_count - group_mean * group_mean
    scaled = (float_feats - group_mean[None, :, None]) * lax.rsqrt(group_var + 1e-05)[None, :, None]
    activated = jax.nn.silu(scaled.reshape(1, row_count, grid_width, channels) * group_gain).astype(
        jnp.bfloat16
    )
    haloed = with_halo(activated, (("sp", 1),), 1)
    padded = jnp.pad(haloed, ((0, 0), (0, 0), (1, 1), (0, 0)))
    conv_sum = conv_taps(padded, conv_weight, row_count, grid_width)
    time_bias = time_embed(timestep, time_weight)
    hidden = (
        features.astype(jnp.float32).reshape(tokens_here, channels) + conv_sum + time_bias
    ).astype(jnp.bfloat16)
    normed = layer_norm(hidden, norm_gain)
    projected = jnp.dot(normed, qkv_weight, preferred_element_type=jnp.float32).astype(jnp.bfloat16)
    head_dim = channels // HEADS
    score_scale = 1.0 / math.sqrt(head_dim)
    split_heads = projected.reshape(tokens_here, HEADS, 3, head_dim)
    queries = split_heads[:, :, 0].transpose(1, 0, 2)
    key_value = split_heads[:, :, 1:].reshape(tokens_here, HEADS * 2 * head_dim)
    all_pairs = lax.all_gather(key_value, "sp", axis=0, tiled=True).reshape(-1, HEADS, 2, head_dim)
    key_rows = all_pairs[:, :, 0].transpose(1, 0, 2)
    value_rows = all_pairs[:, :, 1].transpose(1, 0, 2)
    per_head = lax.map(
        lambda triple: attend_block(triple[0], triple[1], triple[2], score_scale),
        (queries, key_rows, value_rows),
    )
    attended = per_head.astype(jnp.bfloat16).transpose(1, 0, 2).reshape(tokens_here, channels)
    mixed_out = jnp.dot(attended, out_weight, preferred_element_type=jnp.float32)
    updated = (
        (hidden.astype(jnp.float32) + mixed_out)
        .astype(jnp.bfloat16)
        .reshape(1, row_count, grid_width, channels)
    )
    cot_rows = cotangent.reshape(tokens_here, channels)
    local_grad = lax.dot_general(
        attended, cot_rows, (((0,), (0,)), ((), ())), preferred_element_type=jnp.float32
    )
    out_grad = lax.psum(local_grad, ("dp", "sp"))
    return (updated, out_grad)


def solution(mesh):
    in_specs = (
        P("dp", "sp", None, None),
        P("dp"),
        P(),
        P(),
        P(),
        P(),
        P(),
        P(),
        P("dp", "sp", None, None),
    )
    out_specs = (P("dp", "sp", None, None), P())
    return jax.shard_map(
        on_device, mesh=mesh, in_specs=in_specs, out_specs=out_specs, check_vma=False
    )
```

profile of v0, /device:TPU:1, one launch (start us, length us, event | category | flops | bytes accessed | tf_op | source)
XLA Modules:
  0.0 483.0 jit_solution(6016230258676961746)
XLA Ops:
  8.9 29.7 %all-reduce.1 = (f32[32]{0:T(128)S(1)}, f32[32]{0:T(128)S(1)}) all-reduce(f32[32]{0:T(128)S(1)} %reduce_sum.64, f32[32]{0:T(128)S(1)} %reduce_sum.61), channel_id=1, replica_groups=mesh['dp'=16,'sp'=16] {'sp'}, use_global_device_ids=true, to_apply=%region_5.6 | all-reduce | flops 64 | bytes 512 | tf_op jit(solution)/shard_map/psum | solution.py:84
  40.2 2.3 collective-permute-start
  42.6 4.0 collective-permute-start.1
  55.5 2.0 convolution_convert_fusion
  57.5 2.3 copy.12
  59.7 2.0 slice.107
  63.5 70.7 %all-gather.2.cloned.1.call-done = bf16[4096,1280]{0,1:T(8,128)(2,1)} async-done(((bf16[256,1280]{0,1:T(8,128)(2,1)}), bf16[4096,1280]{0,1:T(8,128)(2,1)}) %all-gather.2.cloned.1.call-update) | async-done | bytes 10485776 | tf_op jit(solution)/shard_map/all_gather | solution.py:108
  134.3 9.5 %slice_bitcast_fusion = (bf16[16,4096,40]{1,2,0:T(8,128)(2,1)}, bf16[16,4096,40]{1,2,0:T(8,128)(2,1)}) fusion(bf16[4096,16,2,40]{0,3,2,1:T(8,128)(2,1)} %bitcast.105), kind=kLoop, calls=%fused_computation.15 | loop fusion | bytes 20971520 | tf_op jit(solution)/shard_map/transpose | solution.py:110
  143.8 70.3 %while.10 = (s32[]{:T(128)}, bf16[16,256,40]{1,2,0:T(8,128)(2,1)S(1)}, bf16[16,256,40]{1,2,0:T(8,128)(2,1)}, bf16[16,4096,40]{1,2,0:T(8,128)(2,1)}, bf16[16,4096,40]{1,2,0:T(8,128)(2,1)}, /*index=5*/s32[]{:T(128)}) while((s32[]{:T(128)}, bf16[16,256,40]{1,2,0:T(8,128)(2,1)S(1)}, bf16[16,256,40]{1,2,0:T(8,128)(2,1)}, ...), condition=%wide.region_11.12_spmd, body=%wide.region_8.11_spmd.sunk | while | flops 175111680 | bytes 13306957 | solution.py:111
  146.3 1.9 fusion.78
  150.7 1.9 fusion.78
  152.6 1.8 fusion.76
  155.1 1.9 fusion.78
  159.5 1.9 fusion.78
  161.4 1.8 fusion.76
  163.9 1.9 fusion.78
  168.3 1.9 fusion.78
  170.2 1.8 fusion.76
  172.7 1.9 fusion.78
  177.1 1.9 fusion.78
  181.5 1.9 fusion.78
  185.9 1.9 fusion.78
  190.3 1.9 fusion.78
  194.7 1.9 fusion.78
  199.1 1.9 fusion.78
  203.5 1.9 fusion.78
  207.9 1.9 fusion.78
  212.2 1.9 fusion.78
  214.1 2.6 fusion.54
  216.7 2.3 fusion.16
  219.1 254.4 %all-reduce.4.cloned.1.call-done = f32[640,640]{1,0:T(8,128)} async-done(((f32[640,640]{1,0:T(8,128)}), f32[640,640]{1,0:T(8,128)}) %all-reduce.4.cloned.1.call-update) | async-done | bytes 1638416 | tf_op jit(solution)/shard_map/psum | solution.py:126
  473.4 2.7 copy.30
  (76 shorter events, 48.1 us)
Async XLA Ops:
  7.2 48.3 %copy-start = (bf16[640,1920]{1,0:T(8,128)(2,1)S(1)}, bf16[640,1920]{1,0:T(8,128)(2,1)}, u32[]{:S(2)}) copy-start(bf16[640,1920]{1,0:T(8,128)(2,1)} %param.17) | copy-start | bytes 7372804
  7.2 127.1 %all-gather.2.cloned.1.call-start = ((), (), s32[]{:S(2)}) async-start(), calls=%async_computation | async-start | bytes 11141120 | tf_op jit(solution)/shard_map/all_gather | solution.py:108
  40.2 11.1 %copy-start.1 = (bf16[3,3,640,640]{3,2,1,0:T(8,128)(2,1)S(1)}, bf16[3,3,640,640]{3,2,1,0:T(8,128)(2,1)}, u32[]{:S(2)}) copy-start(bf16[3,3,640,640]{3,2,1,0:T(8,128)(2,1)} %param.14) | copy-start | bytes 22118404
  40.2 8.3 %collective-permute-start = (bf16[1,1,128,640]{3,2,1,0:T(8,128)(2,1)S(1)}, bf16[1,1,128,640]{3,2,1,0:T(8,128)(2,1)S(1)}, u32[]{:S(2)}, u32[]{:S(2)}) collective-permute-start(bf16[1,1,128,640]{3,2,1,0:T(8,128)(2,1)S(1)} %get-tuple-element.61), channel_id=1, source_target_pairs={{0,1},{1,2},{2,3},{3,4},{4,5},{5,6},{6,7},{7,8},{8,9},{9,10},{10,1... | collective-permute-start | bytes 491528 | tf_op jit(solution)/shard_map/ppermute | solution.py:17
  42.6 6.6 %collective-permute-start.1 = (bf16[1,1,128,640]{3,2,1,0:T(8,128)(2,1)S(1)}, bf16[1,1,128,640]{3,2,1,0:T(8,128)(2,1)S(1)}, u32[]{:S(2)}, u32[]{:S(2)}) collective-permute-start(bf16[1,1,128,640]{3,2,1,0:T(8,128)(2,1)S(1)} %get-tuple-element.62), channel_id=1, source_target_pairs={{1,0},{2,1},{3,2},{4,3},{5,4},{6,5},{7,6},{8,7},{9,8},{10,9},{11,1... | collective-permute-start | bytes 491528 | tf_op jit(solution)/shard_map/ppermute | solution.py:20
  53.2 1.4 copy-start.2
  53.7 1.8 copy-start.3
  61.7 411.7 %all-reduce.4.cloned.1.call-start = ((), (), s32[]{:S(2)}) async-start(), calls=%async_computation.1 | async-start | bytes 3276800 | tf_op jit(solution)/shard_map/psum | solution.py:126
Sparse Core Ops, SparseCore 0:
  61.9 72.3 all-gather.1
  216.8 256.5 all-reduce.3
where the time goes:
time: 486 us; the launch traced here: 483 us
  waiting for transfers between devices  326 us (67%)
  matrix products  72 us (15%)
  blocking collectives  29.7 us (6%)
  local copies, waits for them, and re-layouts  19.1 us (4%)
  between operations  14.9 us (3%)
  other arithmetic  14.8 us (3%)
  starting transfers between devices  6.39 us (1%)
    psum x1, waiting for transfers between devices, on_device(): out_grad = lax.psum(local_grad, ('dp', 'sp'))  254 us
    all_gather x1, waiting for transfers between devices, on_device(): lax.all_gather(key_value, 'sp', axis=0, tiled=True)  70.7 us
    psum x1, blocking collectives, on_device(): lax.psum((jnp.sum(float_feats, axis=(0, 2)), jnp.sum(float_feats * float_...  29.7 us
    dot_general x16, matrix products, attend_block(): jnp.dot(probabilities, value_rows, preferred_element_type=jnp.float32)  29.6 us
    dot_general x16, matrix products, attend_block(): lax.dot_general(queries, key_rows, (((1,), (1,)), ((), ())), preferred_el...  28.9 us
    reduce_sum x16, other arithmetic, attend_block(): jnp.sum(weights, axis=-1, keepdims=True)  11.5 us
  transfers between devices with their start and end apart: 4, of which 3 were waited for; matrix products, arithmetic and copies ran while one was open for 1% of the time, Pallas kernels for 0%

commit v1 on v0

v1 whole, which is shorter than its diff:
```python
import functools
import math

import jax
import jax.numpy as jnp
from jax import lax
from jax.experimental import pallas as pl
from jax.experimental.pallas import tpu as pltpu
from jax.sharding import PartitionSpec as P

HEADS = 16
GROUPS = 32
C = 640
HD = 40
W = 128
TEMB = 320
ROWS = 2
T = ROWS * W
L = 128
HP = 48
NSP = 16
NDP = 16
f32 = jnp.float32
bf16 = jnp.bfloat16
NT = (((1,), (1,)), ((), ()))
TN = (((0,), (0,)), ((), ()))
CK = 512
NC = NSP * T // CK


def split3(v):
    hi = v.astype(bf16).astype(f32)
    rest = v - hi
    mid = rest.astype(bf16).astype(f32)
    return hi, mid, rest - mid


def stack_rows(rows, width):
    r = lax.broadcasted_iota(jnp.int32, (16, width), 0)
    out = jnp.zeros((16, width), f32)
    for i, v in enumerate(rows):
        out = jnp.where(r == i, v, out)
    return out.astype(bf16)


def kernel(
    ts_ref, ggain_ref, ngain_ref, feat_hbm, convw_hbm, timew_hbm, qkvw_hbm, outw_hbm, cot_hbm,
    upd_ref, grad_ref,
    fext, convw, timew, qkvw, outw, cot, wq, wo, cols, hid, stat, xsend, x, s_buf, m_buf,
    at_send, at, g_send, g, rs_send, rs, fin,
    local_sem, stat_ss, stat_rs, halo_ss, halo_rs, x_ss, x_rs, at_ss, at_rs, g_ss, g_rs,
    rs_ss, rs_rs, ag_ss, ag_rs, fin_ss, fin_rs, core_ss,
):
    me = lax.axis_index("sp")
    dp = lax.axis_index("dp")

    def sp_peer(t):
        return lax.rem(me + t, NSP)

    def dp_peer(t):
        return lax.rem(dp + t, NDP)

    def to_sp(src, dst, ss, rs_, j):
        return pltpu.make_async_remote_copy(
            src_ref=src, dst_ref=dst, send_sem=ss, recv_sem=rs_, device_id={"sp": j},
            device_id_type=pl.DeviceIdType.MESH)

    def to_dp(src, dst, ss, rs_, j):
        return pltpu.make_async_remote_copy(
            src_ref=src, dst_ref=dst, send_sem=ss, recv_sem=rs_, device_id={"dp": j},
            device_id_type=pl.DeviceIdType.MESH)

    def loop(lo, hi, body):
        def step(i, c):
            body(i)
            return c
        lax.fori_loop(lo, hi, step, 0)

    barrier = pltpu.get_barrier_semaphore()

    def greet(t):
        pl.semaphore_signal(barrier, inc=1, device_id={"sp": sp_peer(t)},
                            device_id_type=pl.DeviceIdType.MESH)
        pl.semaphore_signal(barrier, inc=1, device_id={"dp": dp_peer(t)},
                            device_id_type=pl.DeviceIdType.MESH)
    loop(1, NSP, greet)

    def fetch(i, src, dst):
        c = pltpu.make_async_copy(src, dst, local_sem.at[i])
        c.start()
        return c
    get_feat = fetch(0, feat_hbm, fext.at[W:W + T])
    get_timew = fetch(1, timew_hbm, timew)
    get_qkvw = fetch(2, qkvw_hbm, qkvw)
    get_convw = fetch(3, convw_hbm, convw)
    get_outw = fetch(4, outw_hbm, outw)
    get_cot = fetch(5, cot_hbm, cot)

    chan = lax.broadcasted_iota(jnp.int32, (C, L), 0)
    grp = lax.broadcasted_iota(jnp.int32, (C, L), 1)
    per_group = C // GROUPS
    member = ((chan >= grp * per_group) & (chan < grp * per_group + per_group))
    member = member.astype(f32).astype(bf16)
    get_feat.wait()
    feats = fext[W:W + T].astype(f32)
    s1 = jnp.sum(feats, axis=0, keepdims=True)
    s2 = jnp.sum(feats * feats, axis=0, keepdims=True)
    parts = jnp.dot(stack_rows(split3(s1) + split3(s2), C), member, preferred_element_type=f32)
    r8 = lax.broadcasted_iota(jnp.int32, (8, L), 0)
    t1 = parts[0:1] + parts[1:2] + parts[2:3]
    t2 = parts[3:4] + parts[4:5] + parts[5:6]
    stat[me] = jnp.where(r8 == 0, t1, jnp.where(r8 == 1, t2, 0.0))

    pl.semaphore_wait(barrier, NSP - 1 + NDP - 1)

    loop(1, NSP, lambda t: to_sp(
        stat.at[me], stat.at[me], stat_ss.at[sp_peer(t)], stat_rs.at[me], sp_peer(t)).start())
    up = to_sp(fext.at[W:2 * W], fext.at[3 * W:4 * W], halo_ss.at[0], halo_rs.at[0],
               lax.max(me - 1, 0))
    down = to_sp(fext.at[2 * W:3 * W], fext.at[0:W], halo_ss.at[1], halo_rs.at[1],
                 lax.min(me + 1, NSP - 1))

    @pl.when(me > 0)
    def _():
        up.start()

    @pl.when(me < NSP - 1)
    def _():
        down.start()

    get_timew.wait()
    half = TEMB // 2
    ti = lax.broadcasted_iota(jnp.int32, (8, TEMB), 1)
    tf = jnp.where(ti < half, ti, ti - half).astype(f32)
    freq = jnp.exp(-math.log(10000.0) * tf / half)
    angle = ts_ref[0].astype(f32) * freq
    emb = jnp.where(ti < half, jnp.cos(angle), jnp.sin(angle))
    emb = emb / (1.0 + jnp.exp(-emb))
    time_bias = jnp.dot(emb.astype(bf16), timew[...], preferred_element_type=f32)[0:1]

    get_qkvw.wait()
    lane = lax.broadcasted_iota(jnp.int32, (1, L), 1)
    for j in range(HEADS):
        base = (3 * HD * j) // L * L
        off = 3 * HD * j - base
        if off == 0:
            piece = qkvw[:, base:base + L].astype(f32)
        elif base + 2 * L <= 3 * C:
            piece = pltpu.roll(qkvw[:, base:base + 2 * L].astype(f32), 2 * L - off, axis=1)[:, :L]
        else:
            piece = pltpu.roll(qkvw[:, base:base + L].astype(f32), L - off, axis=1)
        piece = jnp.where(lane < 3 * HD, piece, 0.0).astype(bf16)
        wq[j // 2, :, (j % 2) * L:(j % 2) * L + L] = piece
    get_outw.wait()
    for j in range(HEADS):
        if (HD * j) % 16 == 0:
            rows = outw[HD * j:HD * j + HP] if j < HEADS - 1 else outw[HD * j:HD * j + HD]
            rows = rows.astype(f32)[:HD]
        else:
            rows = outw[HD * j - 8:HD * j + HD].astype(f32)[8:]
        wo[HP * j:HP * j + HP] = jnp.concatenate(
            [rows, jnp.zeros((HP - HD, C), f32)], axis=0).astype(bf16)
    at[me] = jnp.zeros((HP, T), bf16)

    loop(1, NSP, lambda t: to_sp(
        stat.at[sp_peer(t)], stat.at[sp_peer(t)], stat_ss.at[sp_peer(t)],
        stat_rs.at[sp_peer(t)], sp_peer(t)).wait_recv())
    total = jnp.sum(stat[...], axis=0)
    cells = float(NSP * T * per_group)
    mean = total[0:1] / cells
    rstd = lax.rsqrt(total[1:2] / cells - mean * mean + 1e-5)
    chan_t = lax.broadcasted_iota(jnp.int32, (L, C), 1)
    grp_t = lax.broadcasted_iota(jnp.int32, (L, C), 0)
    member_t = ((chan_t >= grp_t * per_group) & (chan_t < grp_t * per_group + per_group))
    member_t = member_t.astype(f32).astype(bf16)
    wide = jnp.dot(stack_rows(split3(mean) + split3(rstd), L), member_t,
                   preferred_element_type=f32)
    mean_c = wide[0:1] + wide[1:2] + wide[2:3]
    rstd_c = wide[3:4] + wide[4:5] + wide[5:6]
    col = lax.broadcasted_iota(jnp.int32, (W, C), 0)

    def activate(r, keep):
        v = (fext[r * W:(r + 1) * W].astype(f32) - mean_c) * rstd_c * ggain_ref[...]
        a = v / (1.0 + jnp.exp(-v))
        if keep is not None:
            a = jnp.where(keep, a, 0.0)
        here = slice(r * W, (r + 1) * W)
        cols[here, 0:C] = jnp.where(col == 0, 0.0, pltpu.roll(a, 1, axis=0)).astype(bf16)
        cols[here, C:2 * C] = a.astype(bf16)
        cols[here, 2 * C:3 * C] = jnp.where(
            col == W - 1, 0.0, pltpu.roll(a, W - 1, axis=0)).astype(bf16)

    activate(1, None)
    activate(2, None)

    @pl.when(me > 0)
    def _():
        down.wait_recv()

    @pl.when(me == 0)
    def _():
        fext[0:W] = jnp.zeros((W, C), bf16)

    @pl.when(me < NSP - 1)
    def _():
        up.wait_recv()

    @pl.when(me == NSP - 1)
    def _():
        fext[3 * W:4 * W] = jnp.zeros((W, C), bf16)

    activate(0, me > 0)
    activate(3, me < NSP - 1)

    get_convw.wait()
    conv = fext[W:W + T].astype(f32) + time_bias
    for a in range(3):
        conv = conv + jnp.dot(cols[a * W:a * W + T], convw[a], preferred_element_type=f32)
    hidden = conv.astype(bf16)
    hid[...] = hidden
    h = hidden.astype(f32)
    centred = h - jnp.mean(h, axis=1, keepdims=True)
    variance = jnp.mean(centred * centred, axis=1, keepdims=True)
    normed = (centred * lax.rsqrt(variance + 1e-5) * ngain_ref[...]).astype(bf16)

    scale = jnp.where(lane < HD, math.log2(math.e) / math.sqrt(HD), 1.0)
    ones = jnp.where(lane >= 3 * HD, 1.0, 0.0)

    def send_x(j):
        return to_sp(xsend.at[j], x.at[me], x_ss.at[j], x_rs.at[me], j)

    def project(u):
        chip = lax.rem(me // 2 + u, NSP // 2)
        pair = jnp.dot(normed, wq[chip], preferred_element_type=f32)
        for k in range(2):
            xsend[2 * chip + k] = (pair[:, k * L:(k + 1) * L] * scale + ones).astype(bf16)
        for k in range(2):
            @pl.when(2 * chip + k != me)
            def _():
                send_x(2 * chip + k).start()
    loop(0, NSP // 2, project)
    x[me] = xsend[me]

    def recv_x(t):
        j = sp_peer(t)
        to_sp(x.at[j], x.at[j], x_ss.at[j], x_rs.at[j], j).wait_recv()
    loop(1, NSP, recv_x)
    get_cot.wait()

    def query(j):
        q = pltpu.roll(x[j].astype(f32), HD, axis=1)
        return jnp.where((lane >= HD) & (lane < 2 * HD), q, 0.0).astype(bf16)

    def keys(c):
        per = CK // T
        return x[c * per:(c + 1) * per].reshape(CK, L)

    def scores(q, buf, c, top):
        s = lax.dot_general(q, keys(c), NT, preferred_element_type=f32)
        s_buf[buf, :, c * CK:(c + 1) * CK] = s
        for i in range(CK // L):
            top = jnp.maximum(top, s[:, i * L:(i + 1) * L])
        return top

    def weigh(m, buf, c, z):
        p = jnp.exp2(s_buf[buf, :, c * CK:(c + 1) * CK] - m).astype(bf16)
        return z + jnp.dot(p, keys(c), preferred_element_type=f32)

    lowest = jnp.full((T, L), -jnp.inf, f32)
    hrow = lax.broadcasted_iota(jnp.int32, (HP, T), 0)

    def attend(t, cur, nxt):
        m = jnp.max(m_buf[...], axis=1, keepdims=True)
        q = query(sp_peer(t + 2))
        top = lowest
        z = jnp.zeros((T, L), f32)
        for c in range(NC):
            top = scores(q, nxt, c, top)
            z = weigh(m, cur, c, z)
        m_buf[...] = top
        zt = (z / z[:, 3 * HD:3 * HD + 1]).T[2 * HD:]
        return jnp.where(hrow < HD, zt, 0.0).astype(bf16)

    def send_at(j):
        return to_sp(at_send.at[j], at.at[me], at_ss.at[j], at_rs.at[me], j)

    def recv_at(j):
        return to_sp(at.at[j], at.at[j], at_ss.at[j], at_rs.at[j], j)

    def send_g(j):
        return to_sp(g_send.at[j], g.at[me], g_ss.at[j], g_rs.at[me], j)

    def source(t):
        return lax.rem(me + 2 * NSP - 1 - t, NSP)

    top = lowest
    q0 = query(sp_peer(1))
    for c in range(NC):
        top = scores(q0, 0, c, top)
    m_buf[...] = top

    def two_steps(u):
        t = 2 * u
        first = lax.select(u >= 2, source(t - 4), me)
        second = lax.select(u >= 2, source(t - 3), me)

        @pl.when(u >= 2)
        def _():
            recv_at(first).wait_recv()
            recv_at(second).wait_recv()

        block = jnp.concatenate([at[first], at[second]], axis=0)
        both = jnp.dot(block, cot[...], preferred_element_type=f32).astype(bf16)
        g_send[first] = both[:HP]
        g_send[second] = both[HP:]
        at_send[sp_peer(t + 1)] = attend(t, 0, 1)
        send_at(sp_peer(t + 1)).start()

        @pl.when(u >= 2)
        def _():
            send_g(first).start()
            send_g(second).start()

        at_send[sp_peer(t + 2)] = attend(t + 1, 1, 0)

        @pl.when(u < NSP // 2 - 1)
        def _():
            send_at(sp_peer(t + 2)).start()
    loop(0, NSP // 2, two_steps)

    at[me] = at_send[me]
    last = [source(t) for t in range(12, 15)]
    for j in last:
        recv_at(j).wait_recv()
    block = jnp.concatenate([at[j] for j in last] + [at[me]], axis=0)
    final = jnp.dot(block, cot[...], preferred_element_type=f32).astype(bf16)
    for i, j in enumerate(last):
        g_send[j] = final[i * HP:(i + 1) * HP]
        send_g(j).start()
    g[me] = final[3 * HP:]

    mixed = lax.dot_general(at[...].reshape(NSP * HP, T), wo[...], TN, preferred_element_type=f32)
    upd_ref[...] = (hid[...].astype(f32) + mixed).astype(bf16)

    def recv_g(t):
        j = sp_peer(t)
        to_sp(g.at[j], g.at[j], g_ss.at[j], g_rs.at[j], j).wait_recv()
    loop(1, NSP, recv_g)
    here = jnp.zeros((HP, C), f32)
    for j in range(NSP):
        here = here + g[j].astype(f32)
    here = here.astype(bf16)
    for i in range(15):
        rs_send[i] = here[16 * (i // 5):16 * (i // 5) + 16, L * (i % 5):L * (i % 5) + L]
    rs_send[15] = jnp.zeros((16, L), bf16)

    def send_rs(t):
        j = dp_peer(t)
        return to_dp(rs_send.at[j], rs.at[dp], rs_ss.at[j], rs_rs.at[dp], j)
    loop(1, NDP, lambda t: send_rs(t).start())
    rs[dp] = rs_send[dp]

    def recv_rs(t):
        j = dp_peer(t)
        to_dp(rs.at[j], rs.at[j], rs_ss.at[j], rs_rs.at[j], j).wait_recv()
    loop(1, NDP, recv_rs)
    fin[me, dp] = jnp.sum(rs[...].astype(f32), axis=0).astype(bf16)

    def send_ag(t):
        j = dp_peer(t)
        return to_dp(fin.at[me, dp], fin.at[me, dp], ag_ss.at[j], ag_rs.at[dp], j)
    loop(1, NDP, lambda t: send_ag(t).start())

    def recv_ag(t):
        j = dp_peer(t)
        to_dp(fin.at[me, j], fin.at[me, j], ag_ss.at[j], ag_rs.at[j], j).wait_recv()
    loop(1, NDP, recv_ag)

    sibling = me + 1 - 2 * lax.rem(me, 2)

    def send_fin(u):
        j = lax.rem(me + 2 * u, NSP)
        return to_sp(fin.at[me], fin.at[me], fin_ss.at[j], fin_rs.at[me], j)

    def pass_on(j):
        return to_sp(fin.at[j], fin.at[j], core_ss.at[j], fin_rs.at[j], sibling)
    loop(1, NSP // 2, lambda u: send_fin(u).start())
    pass_on(me).start()

    def relay(u):
        j = lax.rem(me + NSP - 2 * u, NSP)
        to_sp(fin.at[j], fin.at[j], fin_ss.at[j], fin_rs.at[j], j).wait_recv()
        pass_on(j).start()
    loop(1, NSP // 2, relay)

    def recv_core(u):
        j = lax.rem(sibling + NSP - 2 * u, NSP)
        to_sp(fin.at[j], fin.at[j], core_ss.at[j], fin_rs.at[j], sibling).wait_recv()
    loop(0, NSP // 2, recv_core)

    for j in range(HEADS):
        for i in range(15):
            a, b = i // 5, i % 5
            grad_ref[HP * j + 16 * a:HP * j + 16 * a + 16, L * b:L * b + L] = fin[j, i]

    @pl.when(me > 0)
    def _():
        up.wait_send()

    @pl.when(me < NSP - 1)
    def _():
        down.wait_send()

    def drain(t):
        j = sp_peer(t)
        to_sp(stat.at[me], stat.at[me], stat_ss.at[j], stat_rs.at[me], j).wait_send()
        send_x(j).wait_send()
        send_at(j).wait_send()
        send_g(j).wait_send()
        send_rs(t).wait_send()
        send_ag(t).wait_send()
    loop(1, NSP, drain)

    def drain_fin(u):
        send_fin(u).wait_send()
        pass_on(lax.rem(me + NSP - 2 * u, NSP)).wait_send()
    loop(1, NSP // 2, drain_fin)
    pass_on(me).wait_send()


def on_device(features, timestep, group_gain, conv_weight, time_weight, norm_gain, qkv_weight,
              out_weight, cotangent):
    vmem = pl.BlockSpec(memory_space=pltpu.VMEM)
    hbm = pl.BlockSpec(memory_space=pl.ANY)
    dma = pltpu.SemaphoreType.DMA
    updated, grad = pl.pallas_call(
        kernel,
        out_shape=(
            jax.ShapeDtypeStruct((T, C), bf16),
            jax.ShapeDtypeStruct((HEADS * HP, C), bf16),
        ),
        in_specs=[pl.BlockSpec(memory_space=pltpu.SMEM), vmem, vmem] + [hbm] * 6,
        out_specs=(vmem, vmem),
        scratch_shapes=[
            pltpu.VMEM((4 * W, C), bf16),
            pltpu.VMEM((3, 3 * C, C), bf16),
            pltpu.VMEM((TEMB, C), bf16),
            pltpu.VMEM((C, 3 * C), bf16),
            pltpu.VMEM((C, C), bf16),
            pltpu.VMEM((T, C), bf16),
            pltpu.VMEM((HEADS // 2, C, 2 * L), bf16),
            pltpu.VMEM((HEADS * HP, C), bf16),
            pltpu.VMEM((4 * W, 3 * C), bf16),
            pltpu.VMEM((T, C), bf16),
            pltpu.VMEM((NSP, 8, L), f32),
            pltpu.VMEM((NSP, T, L), bf16),
            pltpu.VMEM((NSP, T, L), bf16),
            pltpu.VMEM((2, T, NSP * T), f32),
            pltpu.VMEM((T, L), f32),
            pltpu.VMEM((NSP, HP, T), bf16),
            pltpu.VMEM((NSP, HP, T), bf16),
            pltpu.VMEM((NSP, HP, C), bf16),
            pltpu.VMEM((NSP, HP, C), bf16),
            pltpu.VMEM((NDP, 16, L), bf16),
            pltpu.VMEM((NDP, 16, L), bf16),
            pltpu.VMEM((NSP, NDP, 16, L), bf16),
            dma((6,)), dma((16,)), dma((16,)), dma((2,)), dma((2,)), dma((16,)), dma((16,)),
            dma((16,)), dma((16,)), dma((16,)), dma((16,)), dma((16,)), dma((16,)),
            dma((16,)), dma((16,)), dma((16,)), dma((16,)), dma((16,)),
        ],
        compiler_params=pltpu.CompilerParams(
            collective_id=0, has_side_effects=True, vmem_limit_bytes=60 * 2**20),
        name="level",
    )(
        timestep, group_gain.reshape(1, C), norm_gain.reshape(1, C), features.reshape(T, C),
        conv_weight.reshape(3, 3 * C, C), time_weight, qkv_weight, out_weight,
        cotangent.reshape(T, C),
    )
    out_grad = grad.reshape(HEADS, HP, C)[:, :HD].reshape(C, C).astype(f32)
    return updated.reshape(1, ROWS, W, C), out_grad


def solution(mesh):
    slab = P("dp", "sp", None, None)
    return jax.shard_map(
        on_device, mesh=mesh,
        in_specs=(slab, P("dp"), P(), P(), P(), P(), P(), P(), slab),
        out_specs=(slab, P()), check_vma=False,
    )
```

time: 486 us -> 101 us (0.21)
  waiting for transfers between devices: 326 us -> 0 us
  Pallas kernels: 0 us -> 93.7 us
  matrix products: 72 us -> 0 us
  blocking collectives: 29.7 us -> 0 us
  local copies, waits for them, and re-layouts: 19.1 us -> 4.53 us
  between operations: 14.9 us -> 1.3 us
  other arithmetic: 14.8 us -> 1.35 us
  starting transfers between devices: 6.39 us -> 0 us
    psum x1 -> x0, waiting for transfers between devices: 254 us -> none  [on_device(): out_grad = lax.psum(local_grad, ('dp', 'sp'))]
    pallas_call x0 -> x1, Pallas kernels: none -> 93.7 us  [on_device(): pl.pallas_call(kernel, out_shape=(jax.ShapeDtypeStruct((T, C), bf16), jax...]
    dot_general x45 -> x0, matrix products: 72 us -> none  [the longest x16 29.6 us: attend_block(): jnp.dot(probabilities, value_rows, preferred_element_type=jnp.float32)]
    all_gather x1 -> x0, waiting for transfers between devices: 70.7 us -> none  [on_device(): lax.all_gather(key_value, 'sp', axis=0, tiled=True)]
    psum x1 -> x0, blocking collectives: 29.7 us -> none  [on_device(): lax.psum((jnp.sum(float_feats, axis=(0, 2)), jnp.sum(float_feats * float_...]
    reduce_sum x20 -> x0, other arithmetic: 13.2 us -> none  [the longest x16 11.5 us: attend_block(): jnp.sum(weights, axis=-1, keepdims=True)]
    transpose x2 -> x0, local copies, waits for them, and re-layouts: 11.3 us -> none  [the longest x1 9.54 us: on_device(): value_rows = all_pairs[:, :, 1].transpose(1, 0, 2)]
    ppermute x2 -> x0, starting transfers between devices: 6.31 us -> none  [the longest x1 4 us: with_halo(): lax.ppermute(lax.slice_in_dim(block, 0, width, axis=dim), axis, backward)]
  transfers between devices with their start and end apart: 4 -> 0, of which waited for: 3 -> 0; matrix products, arithmetic and copies ran while one was open for 1% -> 0% of each run, Pallas kernels for 0% -> 0%
where the time goes in v1:
time: 101 us
  Pallas kernels  93.7 us (93%)
  local copies, waits for them, and re-layouts  4.53 us (4%)
  other arithmetic  1.35 us (1%)
  between operations  1.3 us (1%)
    pallas_call x1, Pallas kernels, on_device(): pl.pallas_call(kernel, out_shape=(jax.ShapeDtypeStruct((T, C), bf16), jax...  93.7 us

profile of v1, /device:TPU:1, one launch (start us, length us, event | category | flops | bytes accessed | tf_op | source)
XLA Modules:
  0.0 100.9 jit_solution(4980709752791123109)
XLA Ops:
  1.3 1.3 %reshape.28.ggain_ref = f32[1,640]{1,0:T(1,128)} reshape(f32[640]{0:T(1024)} %param.11) | data formatting | bytes 5120 | tf_op jit(solution)/shard_map/reshape | solution.py:475
  2.5 1.3 %reshape.29.ngain_ref = f32[1,640]{1,0:T(1,128)} reshape(f32[640]{0:T(1024)} %param.14) | data formatting | bytes 5120 | tf_op jit(solution)/shard_map/reshape | solution.py:475
  3.8 93.7 %level.1 = (bf16[256,640]{1,0:T(8,128)(2,1)}, bf16[768,640]{1,0:T(8,128)(2,1)}) custom-call(s32[1]{0:T(128)S(6)} %copy.12.ts_ref, f32[1,640]{1,0:T(1,128)} %reshape.28.ggain_ref, f32[1,640]{1,0:T(1,128)} %reshape.29.ngain_ref, bf16[256,640]{1,0:T(8,128)(2,1)} %bitcast.10, bf16[3,1920,640]{2,1,0:T(8,128)(2,1)} %bitcast.8, bf16[320,640]{1,0:T(8,128)(2,1)} %timew_hbm.1, ...), custom_call_target="tpu_custom_call" | custom-call | tf_op jit(solution)/shard_map/level/pallas_call | solution.py:436
  97.6 0.0 copy-start
  97.6 1.3 %slice.4 = bf16[16,40,640]{2,1,0:T(8,128)(2,1)S(1)} slice(bf16[16,48,640]{2,1,0:T(8,128)(2,1)} %bitcast.9), slice={[0:16], [0:40], [0:640]} | slice | bytes 1638400 | tf_op jit(solution)/shard_map/slice | solution.py:479
  98.8 1.3 %bitcast_convert_fusion = f32[640,640]{1,0:T(8,128)} fusion(bf16[16,40,640]{2,1,0:T(8,128)(2,1)S(1)} %slice.4), kind=kLoop, calls=%fused_computation | loop fusion | flops 409600 | bytes 2457600 | tf_op jit(solution)/shard_map/convert_element_type | solution.py:479
  100.2 0.0 copy-done
  100.2 0.7 copy.13
Async XLA Ops:
  97.6 2.6 %copy-start = (bf16[256,640]{1,0:T(8,128)(2,1)S(1)}, bf16[256,640]{1,0:T(8,128)(2,1)}, u32[]{:S(2)}) copy-start(bf16[256,640]{1,0:T(8,128)(2,1)} %get-tuple-element.4) | copy-start | bytes 983044

commit v2 on v1

v2 whole, which is shorter than its diff:
```python
import functools
import math

import jax
import jax.numpy as jnp
from jax import lax
from jax.experimental import pallas as pl
from jax.experimental.pallas import tpu as pltpu
from jax.sharding import PartitionSpec as P

HEADS = 16
GROUPS = 32
C = 640
HD = 40
W = 128
TEMB = 320
ROWS = 2
T = ROWS * W
L = 128
HP = 48
NSP = 16
NDP = 16
f32 = jnp.float32
bf16 = jnp.bfloat16
NT = (((1,), (1,)), ((), ()))
TN = (((0,), (0,)), ((), ()))
CK = 512


def split3(v):
    hi = v.astype(bf16).astype(f32)
    rest = v - hi
    mid = rest.astype(bf16).astype(f32)
    return hi, mid, rest - mid


def stack_rows(rows, width):
    r = lax.broadcasted_iota(jnp.int32, (16, width), 0)
    out = jnp.zeros((16, width), f32)
    for i, v in enumerate(rows):
        out = jnp.where(r == i, v, out)
    return out.astype(bf16)


def kernel(
    ts_ref, ggain_ref, ngain_ref, feat_hbm, convw_hbm, timew_hbm, qkvw_hbm, outw_hbm, cot_hbm,
    upd_ref, grad_ref,
    fext, convw, timew, qkvw, outw, cot, wq, wo, cols, hid, stat, xsend, x, s_buf, m_buf,
    at_send, at, g_send, g, part, other, rs_send, rs, zs, fin, z_own, m_own,
    local_sem, stat_ss, stat_rs, halo_ss, halo_rs, x_ss, x_rs, at_ss, at_rs, g_ss, g_rs,
    cot_ss, cot_rs, part_ss, part_rs, rs_ss, rs_rs, zs_ss, zs_rs, ag_ss, ag_rs, fin_ss, fin_rs, rest_ss, rest_rs, core_ss, core_rs,
):
    me = lax.axis_index("sp")
    dp = lax.axis_index("dp")

    def sp_peer(t):
        return lax.rem(me + t, NSP)

    y, z, core = me // 4, lax.rem(me // 2, 2), lax.rem(me, 2)
    zh, xi = dp // 4, lax.rem(dp, 4)

    chip = me // 2

    def x_peer(t):
        return zh * 4 + lax.rem(xi + t, 4)

    def zh_peer(t):
        return lax.rem(zh + t, 4) * 4 + xi

    def slab(dy, dz, dc):
        return lax.rem(y + dy, 4) * 4 + lax.rem(z + dz, 2) * 2 + lax.rem(core + dc, 2)

    def to_sp(src, dst, ss, rs_, j):
        return pltpu.make_async_remote_copy(
            src_ref=src, dst_ref=dst, send_sem=ss, recv_sem=rs_, device_id={"sp": j},
            device_id_type=pl.DeviceIdType.MESH)

    def to_dp(src, dst, ss, rs_, j):
        return pltpu.make_async_remote_copy(
            src_ref=src, dst_ref=dst, send_sem=ss, recv_sem=rs_, device_id={"dp": j},
            device_id_type=pl.DeviceIdType.MESH)

    def loop(lo, hi, body):
        def step(i, c):
            body(i)
            return c
        lax.fori_loop(lo, hi, step, 0)

    barrier = pltpu.get_barrier_semaphore()

    def greet(t):
        pl.semaphore_signal(barrier, inc=1, device_id={"sp": sp_peer(t)},
                            device_id_type=pl.DeviceIdType.MESH)

    for t in range(1, 4):
        for j in (zh_peer(t), x_peer(t)):
            pl.semaphore_signal(barrier, inc=1, device_id={"dp": j},
                                device_id_type=pl.DeviceIdType.MESH)
    loop(1, NSP, greet)

    def fetch(i, src, dst):
        c = pltpu.make_async_copy(src, dst, local_sem.at[i])
        c.start()
        return c
    get_feat = fetch(0, feat_hbm, fext.at[W:W + T])

    chan = lax.broadcasted_iota(jnp.int32, (C, L), 0)
    grp = lax.broadcasted_iota(jnp.int32, (C, L), 1)
    per_group = C // GROUPS
    member = ((chan >= grp * per_group) & (chan < grp * per_group + per_group))
    member = member.astype(f32).astype(bf16)
    get_feat.wait()
    get_timew = fetch(1, timew_hbm, timew)
    get_qkvw = fetch(2, qkvw_hbm, qkvw)
    get_outw = fetch(4, outw_hbm, outw)
    get_convw = fetch(3, convw_hbm, convw)
    get_cot = fetch(5, cot_hbm, cot.at[core])
    feats = fext[W:W + T].astype(f32)
    s1 = jnp.sum(feats, axis=0, keepdims=True)
    s2 = jnp.sum(feats * feats, axis=0, keepdims=True)
    parts = jnp.dot(stack_rows(split3(s1) + split3(s2), C), member, preferred_element_type=f32)
    r8 = lax.broadcasted_iota(jnp.int32, (8, L), 0)
    t1 = parts[0:1] + parts[1:2] + parts[2:3]
    t2 = parts[3:4] + parts[4:5] + parts[5:6]
    stat[me] = jnp.where(r8 == 0, t1, jnp.where(r8 == 1, t2, 0.0))

    pl.semaphore_wait(barrier, NSP - 1 + 3 + 3)

    loop(1, NSP, lambda t: to_sp(
        stat.at[me], stat.at[me], stat_ss.at[sp_peer(t)], stat_rs.at[me], sp_peer(t)).start())
    up = to_sp(fext.at[W:2 * W], fext.at[3 * W:4 * W], halo_ss.at[0], halo_rs.at[0],
               lax.max(me - 1, 0))
    down = to_sp(fext.at[2 * W:3 * W], fext.at[0:W], halo_ss.at[1], halo_rs.at[1],
                 lax.min(me + 1, NSP - 1))

    @pl.when(me > 0)
    def _():
        up.start()

    @pl.when(me < NSP - 1)
    def _():
        down.start()

    sibling = slab(0, 0, 1)
    swap_cot = to_sp(cot.at[core], cot.at[core], cot_ss.at[0], cot_rs.at[0], sibling)

    get_timew.wait()
    half = TEMB // 2
    ti = lax.broadcasted_iota(jnp.int32, (8, TEMB), 1)
    tf = jnp.where(ti < half, ti, ti - half).astype(f32)
    freq = jnp.exp(-math.log(10000.0) * tf / half)
    angle = ts_ref[...].astype(f32).reshape(1, 1) * freq
    emb = jnp.where(ti < half, jnp.cos(angle), jnp.sin(angle))
    emb = emb / (1.0 + jnp.exp(-emb))
    time_bias = jnp.dot(emb.astype(bf16), timew[...], preferred_element_type=f32)[0:1]

    get_qkvw.wait()
    lane = lax.broadcasted_iota(jnp.int32, (1, L), 1)
    for j in range(HEADS):
        base = (3 * HD * j) // L * L
        off = 3 * HD * j - base
        if off == 0:
            piece = qkvw[:, base:base + L].astype(f32)
        elif base + 2 * L <= 3 * C:
            piece = pltpu.roll(qkvw[:, base:base + 2 * L].astype(f32), 2 * L - off, axis=1)[:, :L]
        else:
            piece = pltpu.roll(qkvw[:, base:base + L].astype(f32), L - off, axis=1)
        piece = jnp.where(lane < 3 * HD, piece, 0.0).astype(bf16)
        wq[j // 2, :, (j % 2) * L:(j % 2) * L + L] = piece
    get_outw.wait()
    for j in range(HEADS):
        if (HD * j) % 16 == 0:
            rows = outw[HD * j:HD * j + HP] if j < HEADS - 1 else outw[HD * j:HD * j + HD]
            rows = rows.astype(f32)[:HD]
        else:
            rows = outw[HD * j - 8:HD * j + HD].astype(f32)[8:]
        here = slice(HP * (j // 2), HP * (j // 2) + HP)
        wo[j % 2, here] = jnp.concatenate(
            [rows, jnp.zeros((HP - HD, C), f32)], axis=0).astype(bf16)
    at[chip] = jnp.zeros((HP, 2 * T), bf16)

    loop(1, NSP, lambda t: to_sp(
        stat.at[sp_peer(t)], stat.at[sp_peer(t)], stat_ss.at[sp_peer(t)],
        stat_rs.at[sp_peer(t)], sp_peer(t)).wait_recv())
    total = jnp.sum(stat[...], axis=0)
    cells = float(NSP * T * per_group)
    mean = total[0:1] / cells
    rstd = lax.rsqrt(total[1:2] / cells - mean * mean + 1e-5)
    chan_t = lax.broadcasted_iota(jnp.int32, (L, C), 1)
    grp_t = lax.broadcasted_iota(jnp.int32, (L, C), 0)
    member_t = ((chan_t >= grp_t * per_group) & (chan_t < grp_t * per_group + per_group))
    member_t = member_t.astype(f32).astype(bf16)
    wide = jnp.dot(stack_rows(split3(mean) + split3(rstd), L), member_t,
                   preferred_element_type=f32)
    mean_c = wide[0:1] + wide[1:2] + wide[2:3]
    rstd_c = wide[3:4] + wide[4:5] + wide[5:6]
    col = lax.broadcasted_iota(jnp.int32, (W, C), 0)

    def activate(r, keep):
        v = (fext[r * W:(r + 1) * W].astype(f32) - mean_c) * rstd_c * ggain_ref[...].reshape(1, C)
        a = v / (1.0 + jnp.exp(-v))
        if keep is not None:
            a = jnp.where(keep, a, 0.0)
        here = slice(r * W, (r + 1) * W)
        cols[here, 0:C] = jnp.where(col == 0, 0.0, pltpu.roll(a, 1, axis=0)).astype(bf16)
        cols[here, C:2 * C] = a.astype(bf16)
        cols[here, 2 * C:3 * C] = jnp.where(
            col == W - 1, 0.0, pltpu.roll(a, W - 1, axis=0)).astype(bf16)

    activate(1, None)
    activate(2, None)

    @pl.when(me > 0)
    def _():
        down.wait_recv()

    @pl.when(me == 0)
    def _():
        fext[0:W] = jnp.zeros((W, C), bf16)

    @pl.when(me < NSP - 1)
    def _():
        up.wait_recv()

    @pl.when(me == NSP - 1)
    def _():
        fext[3 * W:4 * W] = jnp.zeros((W, C), bf16)

    activate(0, me > 0)
    activate(3, me < NSP - 1)

    get_convw.wait()
    get_cot.wait()
    swap_cot.start()
    conv = fext[W:W + T].astype(f32) + time_bias
    for a in range(3):
        conv = conv + jnp.dot(cols[a * W:a * W + T], convw[a], preferred_element_type=f32)
    hidden = conv.astype(bf16)
    hid[...] = hidden
    h = hidden.astype(f32)
    centred = h - jnp.mean(h, axis=1, keepdims=True)
    variance = jnp.mean(centred * centred, axis=1, keepdims=True)
    normed = (centred * lax.rsqrt(variance + 1e-5) * ngain_ref[...].reshape(1, C)).astype(bf16)

    scale = jnp.where(lane < HD, math.log2(math.e) / math.sqrt(HD), 1.0)
    ones = jnp.where(lane >= 3 * HD, 1.0, 0.0)

    def send_x(j):
        return to_sp(xsend.at[j], x.at[me], x_ss.at[j], x_rs.at[me], j)

    for dy, dz in ((0, 1), (1, 0), (3, 0), (2, 0), (0, 0), (1, 1), (3, 1), (2, 1)):
        there = slab(dy, dz, 0) // 2
        pair = jnp.dot(normed, wq[there], preferred_element_type=f32)
        for k in range(2):
            xsend[2 * there + k] = (pair[:, k * L:(k + 1) * L] * scale + ones).astype(bf16)
        if dy == 0 and dz == 0:
            send_x(slab(0, 0, 1)).start()
            x[me] = xsend[me]
        else:
            for k in range(2):
                send_x(2 * there + k).start()

    def recv_x(j):
        to_sp(x.at[j], x.at[j], x_ss.at[j], x_rs.at[j], j).wait_recv()
    for dy in range(4):
        for dc in range(2):
            if dy or dc:
                recv_x(slab(dy, 0, dc))

    def query(j):
        q = pltpu.roll(x[j].astype(f32), HD, axis=1)
        return jnp.where((lane >= HD) & (lane < 2 * HD), q, 0.0).astype(bf16)

    def keys(kind, c):
        first = {"all": 2 * c, "own": 4 * c + 2 * z, "other": 4 * c + 2 * (1 - z)}[kind]
        return x[pl.ds(first, 2)].reshape(2 * T, L)

    chunks = {"all": NSP // 2, "own": NSP // 4, "other": NSP // 4}

    def scores(q, kind, buf, c, top):
        s = lax.dot_general(q, keys(kind, c), NT, preferred_element_type=f32)
        s_buf[buf, :, c * CK:(c + 1) * CK] = s
        for i in range(CK // L):
            top = jnp.maximum(top, s[:, i * L:(i + 1) * L])
        return top

    def weigh(m, kind, buf, c, acc):
        p = jnp.exp2(s_buf[buf, :, c * CK:(c + 1) * CK] - m).astype(bf16)
        return acc + jnp.dot(p, keys(kind, c), preferred_element_type=f32)

    lowest = jnp.full((T, L), -jnp.inf, f32)
    hrow = lax.broadcasted_iota(jnp.int32, (HP, T), 0)

    def begin(q, kind):
        top = lowest
        for c in range(chunks[kind]):
            top = scores(q, kind, 0, c, top)
        m_buf[...] = top

    def attend(kind, buf, nxt, before=None):
        m = jnp.max(m_buf[...], axis=1, keepdims=True)
        if before is None:
            acc = jnp.zeros((T, L), f32)
        else:
            m0 = m_own[before][:, :1]
            m = jnp.maximum(m, m0)
            acc = z_own[before] * jnp.exp2(m0 - m)
        top = lowest
        for c in range(NSP // 2):
            if nxt is not None and c < chunks[nxt[1]]:
                top = scores(nxt[0], nxt[1], 1 - buf, c, top)
            if c < chunks[kind]:
                acc = weigh(m, kind, buf, c, acc)
        if nxt is not None:
            m_buf[...] = top
        return acc, m

    def finish(acc):
        at_t = (acc / acc[:, 3 * HD:3 * HD + 1]).T[2 * HD:]
        return jnp.where(hrow < HD, at_t, 0.0).astype(bf16)

    def dy_of(p):
        k = lax.rem(p, 4)
        return lax.select(k == 0, 2, lax.select(k == 1, 1, lax.select(k == 2, 3, 0)))

    def target(p):
        return slab(dy_of(p), 1 - p // 4, 0) // 2

    def source(p):
        return slab(4 - dy_of(p), 1 - p // 4, 0) // 2

    def send_at(c):
        return to_sp(at_send.at[c], at.at[chip], at_ss.at[c], at_rs.at[chip], 2 * c + core)

    def recv_at(c):
        return to_sp(at.at[c], at.at[c], at_ss.at[c], at_rs.at[c], 2 * c + core)

    def send_g(c):
        return to_sp(g_send.at[c], g.at[chip], g_ss.at[c], g_rs.at[chip], 2 * c + core)

    def i32(v):
        return jnp.int32(v)

    begin(query(2 * target(i32(4))), "own")

    def own_pair(u):
        now, later = target(4 + u), target(4 + lax.rem(u + 1, 4))
        for k in range(2):
            acc, m = attend("own", k, (query(2 * now + 1 if k == 0 else 2 * later), "own"))
            z_own[2 * u + k] = acc
            m_own[2 * u + k] = jnp.broadcast_to(m, (T, L))
    loop(0, 4, own_pair)

    for dy in range(4):
        for dc in range(2):
            recv_x(slab(dy, 1, dc))
    swap_cot.wait_recv()
    cots = cot.reshape(2 * T, C)

    def grads(p, live):
        c = lax.select(live, source(p), chip)

        @pl.when(live)
        def _():
            recv_at(c).wait_recv()

        g_send[c] = jnp.dot(at[c], cots[...], preferred_element_type=f32).astype(bf16)

        def start():
            @pl.when(live)
            def _():
                send_g(c).start()
        return start

    begin(query(2 * target(i32(0))), "all")

    def cross_pair(u, last):
        start = grads(lax.max(u - 2, 0), u >= 2)
        now, later = target(u), target(u + 1)
        acc, _ = attend("all", 0, (query(2 * now + 1), "all"))
        at_send[now, :, 0:T] = finish(acc)
        start()
        acc, _ = attend("all", 1, (query(2 * later), "other" if last else "all"))
        at_send[now, :, T:2 * T] = finish(acc)
        send_at(now).start()
    loop(0, 3, lambda u: cross_pair(u, False))
    cross_pair(i32(3), True)

    def side_pair(u, last):
        start = grads(lax.select(u == 0, 2, u + 1), u != 1)
        now, later = target(4 + u), target(4 + lax.rem(u + 1, 4))
        acc, _ = attend("other", 0, (query(2 * now + 1), "other"), before=2 * u)
        at_send[now, :, 0:T] = finish(acc)
        start()
        acc, _ = attend("other", 1, None if last else (query(2 * later), "other"),
                        before=2 * u + 1)
        at_send[now, :, T:2 * T] = finish(acc)
        if not last:
            send_at(now).start()
    loop(0, 3, lambda u: side_pair(u, False))
    side_pair(i32(3), True)

    at[chip] = at_send[chip]
    last = [source(i32(p)) for p in (5, 6)]
    for c in last:
        recv_at(c).wait_recv()
    block = jnp.concatenate([at[c] for c in last] + [at[chip]], axis=0)
    final = jnp.dot(block, cots[...], preferred_element_type=f32).astype(bf16)
    for i, c in enumerate(last):
        g_send[c] = final[i * HP:(i + 1) * HP]
        send_g(c).start()
    g[chip] = final[2 * HP:]

    mixed = lax.dot_general(at[...].reshape(NSP // 2 * HP, 2 * T), wo[core], TN,
                            preferred_element_type=f32)
    part[0] = mixed[:T]
    part[1] = mixed[T:]
    swap_part = to_sp(part.at[1 - core], other, part_ss.at[0], part_rs.at[0], sibling)
    swap_part.start()

    def recv_g(c):
        to_sp(g.at[c], g.at[c], g_ss.at[c], g_rs.at[c], 2 * c + core).wait_recv()
    loop(1, NSP // 2, lambda t: recv_g(lax.rem(chip + t, NSP // 2)))
    here = jnp.zeros((HP, C), f32)
    for j in range(NSP // 2):
        here = here + g[j].astype(f32)
    here = here.astype(bf16)
    for i in range(16):
        tile = jnp.zeros((16, L), bf16)
        if i < 15:
            tile = here[16 * (i // 5):16 * (i // 5) + 16, L * (i % 5):L * (i % 5) + L]
        rs_send[i // 4, 16 * (i % 4):16 * (i % 4) + 16] = tile

    def send_rs(t):
        k = lax.rem(xi + t, 4)
        return to_dp(rs_send.at[k], rs.at[xi], rs_ss.at[t], rs_rs.at[xi], x_peer(t))

    def send_zs(t):
        return to_dp(zs.at[zh], zs.at[zh], zs_ss.at[t], zs_rs.at[zh], zh_peer(t))
    for t in (2, 1, 3):
        send_rs(t).start()
    rs[xi] = rs_send[xi]
    for t in (1, 3, 2):
        k = lax.rem(xi + t, 4)
        to_dp(rs.at[k], rs.at[k], rs_ss.at[t], rs_rs.at[k], x_peer(t)).wait_recv()
    zs[zh] = jnp.sum(rs[...].astype(f32), axis=0).astype(bf16)
    for t in (2, 1, 3):
        send_zs(t).start()
    for t in (1, 3, 2):
        k = lax.rem(zh + t, 4)
        to_dp(zs.at[k], zs.at[k], zs_ss.at[t], zs_rs.at[k], zh_peer(t)).wait_recv()
    fin[me, 0] = jnp.sum(zs[...].astype(f32), axis=0).astype(bf16)

    def send_ag(t):
        return to_dp(fin.at[me, 0], fin.at[me, 4 - t], ag_ss.at[t], ag_rs.at[4 - t], x_peer(t))

    def send_own(u):
        j = lax.rem(me + 2 * u, NSP)
        return to_sp(fin.at[me, 0], fin.at[me, 0], fin_ss.at[j], fin_rs.at[me], j)

    def send_rest(u):
        j = lax.rem(me + 2 * u, NSP)
        return to_sp(fin.at[me, pl.ds(1, 3)], fin.at[me, pl.ds(1, 3)], rest_ss.at[j],
                     rest_rs.at[me], j)
    def pass_on(j):
        return to_sp(fin.at[j], fin.at[j], core_ss.at[j], core_rs.at[j], sibling)
    for t in (2, 1, 3):
        send_ag(t).start()
    loop(1, NSP // 2, lambda u: send_own(u).start())
    swap_part.wait_recv()
    upd_ref[...] = (hid[...].astype(f32) + part[core] + other[...]).astype(bf16)

    for k in (1, 3, 2):
        to_dp(fin.at[me, k], fin.at[me, k], ag_ss.at[k], ag_rs.at[k], x_peer(k)).wait_recv()
    loop(1, NSP // 2, lambda u: send_rest(u).start())
    pass_on(me).start()

    def relay(u):
        j = lax.rem(me + NSP - 2 * u, NSP)
        to_sp(fin.at[j, 0], fin.at[j, 0], fin_ss.at[j], fin_rs.at[j], j).wait_recv()
        to_sp(fin.at[j, pl.ds(1, 3)], fin.at[j, pl.ds(1, 3)], rest_ss.at[j], rest_rs.at[j],
              j).wait_recv()
        pass_on(j).start()
    loop(1, NSP // 2, relay)

    def recv_core(u):
        j = lax.rem(sibling + NSP - 2 * u, NSP)
        to_sp(fin.at[j], fin.at[j], core_ss.at[j], core_rs.at[j], sibling).wait_recv()
    loop(0, NSP // 2, recv_core)

    quarter = [lax.rem(k + 4 - xi, 4) for k in range(4)]

    def head_rows(j):
        tiles = [fin[j, quarter[i // 4], 16 * (i % 4):16 * (i % 4) + 16] for i in range(15)]
        return jnp.concatenate(
            [jnp.concatenate(tiles[5 * a:5 * a + 5], axis=1) for a in range(3)], axis=0)
    for j in range(0, HEADS, 2):
        two = jnp.concatenate(
            [head_rows(j).astype(f32)[:HD], head_rows(j + 1).astype(f32)[:HD]], axis=0)
        grad_ref[HD * j:HD * j + 2 * HD] = two.astype(bf16)

    @pl.when(me > 0)
    def _():
        up.wait_send()

    @pl.when(me < NSP - 1)
    def _():
        down.wait_send()

    def drain(t):
        j = sp_peer(t)
        to_sp(stat.at[me], stat.at[me], stat_ss.at[j], stat_rs.at[me], j).wait_send()
        send_x(j).wait_send()
    loop(1, NSP, drain)

    def drain_pair(t):
        c = lax.rem(chip + t, NSP // 2)
        send_at(c).wait_send()
        send_g(c).wait_send()
    loop(1, NSP // 2, drain_pair)
    swap_cot.wait_send()
    swap_part.wait_send()
    for t in range(1, 4):
        send_rs(t).wait_send()
        send_zs(t).wait_send()
        send_ag(t).wait_send()

    def drain_fin(u):
        send_own(u).wait_send()
        send_rest(u).wait_send()
        pass_on(lax.rem(me + NSP - 2 * u, NSP)).wait_send()
    loop(1, NSP // 2, drain_fin)
    pass_on(me).wait_send()


def on_device(features, timestep, group_gain, conv_weight, time_weight, norm_gain, qkv_weight,
              out_weight, cotangent):
    vmem = pl.BlockSpec(memory_space=pltpu.VMEM)
    hbm = pl.BlockSpec(memory_space=pl.ANY)
    dma = pltpu.SemaphoreType.DMA
    updated, grad = pl.pallas_call(
        kernel,
        out_shape=(
            jax.ShapeDtypeStruct((T, C), bf16),
            jax.ShapeDtypeStruct((C, C), bf16),
        ),
        in_specs=[vmem, vmem, vmem] + [hbm] * 6,
        out_specs=(vmem, vmem),
        scratch_shapes=[
            pltpu.VMEM((4 * W, C), bf16),
            pltpu.VMEM((3, 3 * C, C), bf16),
            pltpu.VMEM((TEMB, C), bf16),
            pltpu.VMEM((C, 3 * C), bf16),
            pltpu.VMEM((C, C), bf16),
            pltpu.VMEM((2, T, C), bf16),
            pltpu.VMEM((HEADS // 2, C, 2 * L), bf16),
            pltpu.VMEM((2, HEADS // 2 * HP, C), bf16),
            pltpu.VMEM((4 * W, 3 * C), bf16),
            pltpu.VMEM((T, C), bf16),
            pltpu.VMEM((NSP, 8, L), f32),
            pltpu.VMEM((NSP, T, L), bf16),
            pltpu.VMEM((NSP, T, L), bf16),
            pltpu.VMEM((2, T, NSP * T), f32),
            pltpu.VMEM((T, L), f32),
            pltpu.VMEM((NSP // 2, HP, 2 * T), bf16),
            pltpu.VMEM((NSP // 2, HP, 2 * T), bf16),
            pltpu.VMEM((NSP // 2, HP, C), bf16),
            pltpu.VMEM((NSP // 2, HP, C), bf16),
            pltpu.VMEM((2, T, C), f32),
            pltpu.VMEM((T, C), f32),
            pltpu.VMEM((4, 64, L), bf16),
            pltpu.VMEM((4, 64, L), bf16),
            pltpu.VMEM((4, 64, L), bf16),
            pltpu.VMEM((NSP, 4, 64, L), bf16),
            pltpu.VMEM((8, T, L), f32),
            pltpu.VMEM((8, T, L), f32),
            dma((6,)), dma((16,)), dma((16,)), dma((2,)), dma((2,)), dma((16,)), dma((16,)),
            dma((8,)), dma((8,)), dma((8,)), dma((8,)),
            dma((1,)), dma((1,)), dma((1,)), dma((1,)),
            dma((4,)), dma((4,)), dma((4,)), dma((4,)), dma((4,)), dma((4,)),
            dma((16,)), dma((16,)), dma((16,)), dma((16,)), dma((16,)), dma((16,)),
        ],
        compiler_params=pltpu.CompilerParams(
            collective_id=0, has_side_effects=True, vmem_limit_bytes=60 * 2**20),
        name="level",
    )(
        timestep, group_gain, norm_gain, features.reshape(T, C),
        conv_weight.reshape(3, 3 * C, C), time_weight, qkv_weight, out_weight,
        cotangent.reshape(T, C),
    )
    return updated.reshape(1, ROWS, W, C), grad.astype(f32)


def solution(mesh):
    slab = P("dp", "sp", None, None)
    return jax.shard_map(
        on_device, mesh=mesh,
        in_specs=(slab, P("dp"), P(), P(), P(), P(), P(), P(), slab),
        out_specs=(slab, P()), check_vma=False,
    )
```

time: 101 us -> 93.8 us (0.929)
  Pallas kernels: 93.7 us -> 89.1 us
  local copies, waits for them, and re-layouts: 4.53 us -> 0.73 us
  other arithmetic: 1.35 us -> 2.47 us
    pallas_call x1, Pallas kernels: 93.7 us -> 89.1 us  [on_device(): pl.pallas_call(kernel, out_shape=(jax.ShapeDtypeStruct((T, C), bf16), jax...]
    reshape x2 -> x0, local copies, waits for them, and re-layouts: 2.53 us -> none  [the longest x1 1.27 us: on_device(): group_gain.reshape(1, C)]
    slice x1 -> x0, local copies, waits for them, and re-layouts: 1.27 us -> none  [on_device(): out_grad = grad.reshape(HEADS, HP, C)[:, :HD].reshape(C, C).astype(f32)]
    convert_element_type x1, other arithmetic: 1.35 us -> 2.47 us  [on_device(): return (updated.reshape(1, ROWS, W, C), grad.astype(f32))]
where the time goes in v2:
time: 93.8 us; the launch traced here: 93.6 us
  Pallas kernels  89.1 us (95%)
  other arithmetic  2.47 us (3%)
  between operations  1.3 us (1%)
    pallas_call x1, Pallas kernels, on_device(): pl.pallas_call(kernel, out_shape=(jax.ShapeDtypeStruct((T, C), bf16), jax...  89.1 us
    convert_element_type x1, other arithmetic, on_device(): return (updated.reshape(1, ROWS, W, C), grad.astype(f32))  2.47 us

profile of v2, /device:TPU:1, one launch (start us, length us, event | category | flops | bytes accessed | tf_op | source)
XLA Modules:
  0.0 93.6 jit_solution(11850975100362668705)
XLA Ops:
  1.3 89.1 %level.1 = (bf16[256,640]{1,0:T(8,128)(2,1)}, bf16[640,640]{1,0:T(8,128)(2,1)}) custom-call(s32[1]{0:T(128)S(6)} %copy.12.ts_ref, f32[640]{0:T(1024)} %ggain_ref.1, f32[640]{0:T(1024)} %ngain_ref.1, bf16[256,640]{1,0:T(8,128)(2,1)} %bitcast.5, bf16[3,1920,640]{2,1,0:T(8,128)(2,1)} %bitcast.4, bf16[320,640]{1,0:T(8,128)(2,1)} %timew_hbm.1, ...), custom_call_target="tpu_custom_call" | custom-call | tf_op jit(solution)/shard_map/level/pallas_call | solution.py:541
  90.4 0.0 copy-start
  90.4 2.5 %convert_element_type.3 = f32[640,640]{1,0:T(8,128)} convert(bf16[640,640]{1,0:T(8,128)(2,1)} %get-tuple-element.5) | non-fusion elementwise | flops 409600 | bytes 2457600 | tf_op jit(solution)/shard_map/convert_element_type | solution.py:591
  92.9 0.0 copy-done
  92.9 0.7 copy.13
Async XLA Ops:
  90.4 2.5 %copy-start = (bf16[256,640]{1,0:T(8,128)(2,1)S(1)}, bf16[256,640]{1,0:T(8,128)(2,1)}, u32[]{:S(2)}) copy-start(bf16[256,640]{1,0:T(8,128)(2,1)} %get-tuple-element.4) | copy-start | bytes 983044

commit v3 on v2

--- a/solution.py
+++ b/solution.py
@@ -44,11 +44,11 @@
 
 def kernel(
     ts_ref, ggain_ref, ngain_ref, feat_hbm, convw_hbm, timew_hbm, qkvw_hbm, outw_hbm, cot_hbm,
-    upd_ref, grad_ref,
+    upd_ref, fin_out,
     fext, convw, timew, qkvw, outw, cot, wq, wo, cols, hid, stat, xsend, x, s_buf, m_buf,
-    at_send, at, g_send, g, part, other, rs_send, rs, zs, fin, z_own, m_own,
+    at_send, at, g_send, g, part, other, zs, fin, z_own, m_own,
     local_sem, stat_ss, stat_rs, halo_ss, halo_rs, x_ss, x_rs, at_ss, at_rs, g_ss, g_rs,
-    cot_ss, cot_rs, part_ss, part_rs, rs_ss, rs_rs, zs_ss, zs_rs, ag_ss, ag_rs, fin_ss, fin_rs, rest_ss, rest_rs, core_ss, core_rs,
+    cot_ss, cot_rs, part_ss, part_rs, zs_ss, zs_rs, ag_ss, ag_rs, fin_ss, fin_rs, rest_ss, rest_rs, core_ss, core_rs,
 ):
     me = lax.axis_index("sp")
     dp = lax.axis_index("dp")
@@ -93,8 +93,11 @@
                             device_id_type=pl.DeviceIdType.MESH)
 
     for t in range(1, 4):
-        for j in (zh_peer(t), x_peer(t)):
-            pl.semaphore_signal(barrier, inc=1, device_id={"dp": j},
+        pl.semaphore_signal(barrier, inc=1, device_id={"dp": zh_peer(t)},
+                            device_id_type=pl.DeviceIdType.MESH)
+    for t in range(1, 4):
+        for c in range(NSP // 2):
+            pl.semaphore_signal(barrier, inc=1, device_id={"dp": x_peer(t), "sp": 2 * c + core},
                                 device_id_type=pl.DeviceIdType.MESH)
     loop(1, NSP, greet)
 
@@ -124,7 +127,7 @@
     t2 = parts[3:4] + parts[4:5] + parts[5:6]
     stat[me] = jnp.where(r8 == 0, t1, jnp.where(r8 == 1, t2, 0.0))
 
-    pl.semaphore_wait(barrier, NSP - 1 + 3 + 3)
+    pl.semaphore_wait(barrier, NSP - 1 + 3 + 3 * NSP // 2)
 
     loop(1, NSP, lambda t: to_sp(
         stat.at[me], stat.at[me], stat_ss.at[sp_peer(t)], stat_rs.at[me], sp_peer(t)).start())
@@ -156,17 +159,19 @@
 
     get_qkvw.wait()
     lane = lax.broadcasted_iota(jnp.int32, (1, L), 1)
-    for j in range(HEADS):
-        base = (3 * HD * j) // L * L
-        off = 3 * HD * j - base
-        if off == 0:
-            piece = qkvw[:, base:base + L].astype(f32)
-        elif base + 2 * L <= 3 * C:
-            piece = pltpu.roll(qkvw[:, base:base + 2 * L].astype(f32), 2 * L - off, axis=1)[:, :L]
-        else:
-            piece = pltpu.roll(qkvw[:, base:base + L].astype(f32), L - off, axis=1)
-        piece = jnp.where(lane < 3 * HD, piece, 0.0).astype(bf16)
-        wq[j // 2, :, (j % 2) * L:(j % 2) * L + L] = piece
+
+    def regroup(r):
+        here = pl.ds(pl.multiple_of(r * L, L), L)
+        for j in range(HEADS):
+            base = (3 * HD * j) // L * L
+            off = 3 * HD * j - base
+            width = 2 * L if 0 < off and base + 2 * L <= 3 * C else L
+            piece = qkvw[here, base:base + width].astype(f32)
+            if off:
+                piece = pltpu.roll(piece, width - off, axis=1)[:, :L]
+            piece = jnp.where(lane < 3 * HD, piece, 0.0).astype(bf16)
+            wq[j // 2, here, (j % 2) * L:(j % 2) * L + L] = piece
+    loop(0, C // L, regroup)
     get_outw.wait()
     for j in range(HEADS):
         if (HD * j) % 16 == 0:
@@ -178,6 +183,7 @@
         wo[j % 2, here] = jnp.concatenate(
             [rows, jnp.zeros((HP - HD, C), f32)], axis=0).astype(bf16)
     at[chip] = jnp.zeros((HP, 2 * T), bf16)
+    g_send[...] = jnp.zeros(g_send.shape, bf16)
 
     loop(1, NSP, lambda t: to_sp(
         stat.at[sp_peer(t)], stat.at[sp_peer(t)], stat_ss.at[sp_peer(t)],
@@ -197,18 +203,16 @@
     col = lax.broadcasted_iota(jnp.int32, (W, C), 0)
 
     def activate(r, keep):
-        v = (fext[r * W:(r + 1) * W].astype(f32) - mean_c) * rstd_c * ggain_ref[...].reshape(1, C)
+        here = pl.ds(pl.multiple_of(r * W, W), W)
+        v = (fext[here].astype(f32) - mean_c) * rstd_c * ggain_ref[...].reshape(1, C)
         a = v / (1.0 + jnp.exp(-v))
-        if keep is not None:
-            a = jnp.where(keep, a, 0.0)
-        here = slice(r * W, (r + 1) * W)
+        a = jnp.where(keep, a, 0.0)
         cols[here, 0:C] = jnp.where(col == 0, 0.0, pltpu.roll(a, 1, axis=0)).astype(bf16)
         cols[here, C:2 * C] = a.astype(bf16)
         cols[here, 2 * C:3 * C] = jnp.where(
             col == W - 1, 0.0, pltpu.roll(a, W - 1, axis=0)).astype(bf16)
 
-    activate(1, None)
-    activate(2, None)
+    loop(1, 3, lambda r: activate(r, r > 0))
 
     @pl.when(me > 0)
     def _():
@@ -226,8 +230,7 @@
     def _():
         fext[3 * W:4 * W] = jnp.zeros((W, C), bf16)
 
-    activate(0, me > 0)
-    activate(3, me < NSP - 1)
+    loop(0, 2, lambda r: activate(3 * r, jnp.where(r == 0, me > 0, me < NSP - 1)))
 
     get_convw.wait()
     get_cot.wait()
@@ -335,8 +338,17 @@
     def recv_at(c):
         return to_sp(at.at[c], at.at[c], at_ss.at[c], at_rs.at[c], 2 * c + core)
 
-    def send_g(c):
-        return to_sp(g_send.at[c], g.at[chip], g_ss.at[c], g_rs.at[chip], 2 * c + core)
+    def send_g(c, k):
+        return pltpu.make_async_remote_copy(
+            src_ref=g_send.at[c, k], dst_ref=g.at[xi, chip], send_sem=g_ss.at[c, k],
+            recv_sem=g_rs.at[xi, chip], device_id={"dp": zh * 4 + k, "sp": 2 * c + core},
+            device_id_type=pl.DeviceIdType.MESH)
+
+    def put_g(c, rows):
+        for i in range(15):
+            a, b = i // 5, i % 5
+            g_send[c, i // 4, 16 * (i % 4):16 * (i % 4) + 16] = (
+                rows[16 * a:16 * a + 16, L * b:L * b + L])
 
     def i32(v):
         return jnp.int32(v)
@@ -364,52 +376,75 @@
         def _():
             recv_at(c).wait_recv()
 
-        g_send[c] = jnp.dot(at[c], cots[...], preferred_element_type=f32).astype(bf16)
+        put_g(c, jnp.dot(at[c], cots[...], preferred_element_type=f32).astype(bf16))
 
         def start():
             @pl.when(live)
             def _():
-                send_g(c).start()
+                for k in range(4):
+                    send_g(c, k).start()
         return start
 
     begin(query(2 * target(i32(0))), "all")
 
     def cross_pair(u, last):
-        start = grads(lax.max(u - 2, 0), u >= 2)
+        start = grads(i32(0), jnp.bool_(True)) if last else None
         now, later = target(u), target(u + 1)
         acc, _ = attend("all", 0, (query(2 * now + 1), "all"))
         at_send[now, :, 0:T] = finish(acc)
-        start()
         acc, _ = attend("all", 1, (query(2 * later), "other" if last else "all"))
         at_send[now, :, T:2 * T] = finish(acc)
         send_at(now).start()
+        if last:
+            start()
     loop(0, 3, lambda u: cross_pair(u, False))
     cross_pair(i32(3), True)
 
     def side_pair(u, last):
-        start = grads(lax.select(u == 0, 2, u + 1), u != 1)
+        start = grads(lax.select(u == 3, 3, u + 1), u != 2)
         now, later = target(4 + u), target(4 + lax.rem(u + 1, 4))
         acc, _ = attend("other", 0, (query(2 * now + 1), "other"), before=2 * u)
         at_send[now, :, 0:T] = finish(acc)
-        start()
         acc, _ = attend("other", 1, None if last else (query(2 * later), "other"),
                         before=2 * u + 1)
         at_send[now, :, T:2 * T] = finish(acc)
         if not last:
             send_at(now).start()
+        start()
     loop(0, 3, lambda u: side_pair(u, False))
     side_pair(i32(3), True)
 
     at[chip] = at_send[chip]
-    last = [source(i32(p)) for p in (5, 6)]
+    last = [source(i32(p)) for p in (4, 5, 6)]
     for c in last:
         recv_at(c).wait_recv()
     block = jnp.concatenate([at[c] for c in last] + [at[chip]], axis=0)
     final = jnp.dot(block, cots[...], preferred_element_type=f32).astype(bf16)
     for i, c in enumerate(last):
-        g_send[c] = final[i * HP:(i + 1) * HP]
-        send_g(c).start()
-    g[chip] = final[2 * HP:]
+        put_g(c, final[i * HP:(i + 1) * HP])
+        for k in range(4):
+            send_g(c, k).start()
+    put_g(chip, final[3 * HP:])
+    for t in range(1, 4):
+        send_g(chip, lax.rem(xi + t, 4)).start()
+    g[xi, chip] = g_send[chip, xi]
+
+    def recv_g(t):
+        k, c = lax.rem(xi + t // 8, 4), lax.rem(chip + t, 8)
+        pltpu.make_async_remote_copy(
+            src_ref=g.at[k, c], dst_ref=g.at[k, c], send_sem=g_ss.at[c, k],
+            recv_sem=g_rs.at[k, c], device_id={"dp": zh * 4 + k, "sp": 2 * c + core},
+            device_id_type=pl.DeviceIdType.MESH).wait_recv()
+    loop(1, 4 * NSP // 2, recv_g)
+
+    def add_g(k, total):
+        return total + jnp.sum(g[k].astype(f32), axis=0)
+
+    def send_zs(t):
+        return to_dp(zs.at[zh], zs.at[zh], zs_ss.at[t], zs_rs.at[zh], zh_peer(t))
+    zs[zh] = lax.fori_loop(0, 4, add_g, jnp.zeros((64, L), f32)).astype(bf16)
+    for t in (2, 1, 3):
+        send_zs(t).start()
 
     mixed = lax.dot_general(at[...].reshape(NSP // 2 * HP, 2 * T), wo[core], TN,
                             preferred_element_type=f32)
@@ -418,34 +453,6 @@
     swap_part = to_sp(part.at[1 - core], other, part_ss.at[0], part_rs.at[0], sibling)
     swap_part.start()
 
-    def recv_g(c):
-        to_sp(g.at[c], g.at[c], g_ss.at[c], g_rs.at[c], 2 * c + core).wait_recv()
-    loop(1, NSP // 2, lambda t: recv_g(lax.rem(chip + t, NSP // 2)))
-    here = jnp.zeros((HP, C), f32)
-    for j in range(NSP // 2):
-        here = here + g[j].astype(f32)
-    here = here.astype(bf16)
-    for i in range(16):
-        tile = jnp.zeros((16, L), bf16)
-        if i < 15:
-            tile = here[16 * (i // 5):16 * (i // 5) + 16, L * (i % 5):L * (i % 5) + L]
-        rs_send[i // 4, 16 * (i % 4):16 * (i % 4) + 16] = tile
-
-    def send_rs(t):
-        k = lax.rem(xi + t, 4)
-        return to_dp(rs_send.at[k], rs.at[xi], rs_ss.at[t], rs_rs.at[xi], x_peer(t))
-
-    def send_zs(t):
-        return to_dp(zs.at[zh], zs.at[zh], zs_ss.at[t], zs_rs.at[zh], zh_peer(t))
-    for t in (2, 1, 3):
-        send_rs(t).start()
-    rs[xi] = rs_send[xi]
-    for t in (1, 3, 2):
-        k = lax.rem(xi + t, 4)
-        to_dp(rs.at[k], rs.at[k], rs_ss.at[t], rs_rs.at[k], x_peer(t)).wait_recv()
-    zs[zh] = jnp.sum(rs[...].astype(f32), axis=0).astype(bf16)
-    for t in (2, 1, 3):
-        send_zs(t).start()
     for t in (1, 3, 2):
         k = lax.rem(zh + t, 4)
         to_dp(zs.at[k], zs.at[k], zs_ss.at[t], zs_rs.at[k], zh_peer(t)).wait_recv()
@@ -488,16 +495,7 @@
         to_sp(fin.at[j], fin.at[j], core_ss.at[j], core_rs.at[j], sibling).wait_recv()
     loop(0, NSP // 2, recv_core)
 
-    quarter = [lax.rem(k + 4 - xi, 4) for k in range(4)]
-
-    def head_rows(j):
-        tiles = [fin[j, quarter[i // 4], 16 * (i % 4):16 * (i % 4) + 16] for i in range(15)]
-        return jnp.concatenate(
-            [jnp.concatenate(tiles[5 * a:5 * a + 5], axis=1) for a in range(3)], axis=0)
-    for j in range(0, HEADS, 2):
-        two = jnp.concatenate(
-            [head_rows(j).astype(f32)[:HD], head_rows(j + 1).astype(f32)[:HD]], axis=0)
-        grad_ref[HD * j:HD * j + 2 * HD] = two.astype(bf16)
+    fin_out[...] = fin[...]
 
     @pl.when(me > 0)
     def _():
@@ -516,12 +514,13 @@
     def drain_pair(t):
         c = lax.rem(chip + t, NSP // 2)
         send_at(c).wait_send()
-        send_g(c).wait_send()
+        for k in range(4):
+            send_g(c, k).wait_send()
     loop(1, NSP // 2, drain_pair)
     swap_cot.wait_send()
     swap_part.wait_send()
     for t in range(1, 4):
-        send_rs(t).wait_send()
+        send_g(chip, lax.rem(xi + t, 4)).wait_send()
         send_zs(t).wait_send()
         send_ag(t).wait_send()
 
@@ -533,16 +532,48 @@
     pass_on(me).wait_send()
 
 
+def outputs(fin_hbm, upd_hbm, upd_out, grad_out, fin, upd, grad, sem):
+    xi = lax.rem(lax.axis_index("dp"), 4)
+    take = pltpu.make_async_copy(upd_hbm, upd, sem.at[HEADS // 2])
+    move = pltpu.make_async_copy(upd, upd_out, sem.at[HEADS // 2])
+
+    def get(j):
+        return pltpu.make_async_copy(fin_hbm.at[pl.ds(j, 2)], fin.at[pl.ds(j, 2)],
+                                     sem.at[HEADS // 2 + 1 + j // 2])
+    for j in range(0, HEADS, 2):
+        get(j).start()
+    take.start()
+    quarter = [lax.rem(k + 4 - xi, 4) for k in range(4)]
+
+    def head_rows(j):
+        tiles = [fin[j, quarter[i // 4], 16 * (i % 4):16 * (i % 4) + 16] for i in range(15)]
+        return jnp.concatenate(
+            [jnp.concatenate(tiles[5 * a:5 * a + 5], axis=1) for a in range(3)], axis=0)
+    for j in range(0, HEADS, 2):
+        get(j).wait()
+        two = jnp.concatenate(
+            [head_rows(j).astype(f32)[:HD], head_rows(j + 1).astype(f32)[:HD]], axis=0)
+        here = slice(HD * j, HD * j + 2 * HD)
+        grad[here] = two
+        pltpu.make_async_copy(grad.at[here], grad_out.at[here], sem.at[j // 2]).start()
+    take.wait()
+    move.start()
+    for j in range(0, HEADS, 2):
+        here = slice(HD * j, HD * j + 2 * HD)
+        pltpu.make_async_copy(grad.at[here], grad_out.at[here], sem.at[j // 2]).wait()
+    move.wait()
+
+
 def on_device(features, timestep, group_gain, conv_weight, time_weight, norm_gain, qkv_weight,
               out_weight, cotangent):
     vmem = pl.BlockSpec(memory_space=pltpu.VMEM)
     hbm = pl.BlockSpec(memory_space=pl.ANY)
     dma = pltpu.SemaphoreType.DMA
-    updated, grad = pl.pallas_call(
+    updated, tiles = pl.pallas_call(
         kernel,
         out_shape=(
             jax.ShapeDtypeStruct((T, C), bf16),
-            jax.ShapeDtypeStruct((C, C), bf16),
+            jax.ShapeDtypeStruct((NSP, 4, 64, L), bf16),
         ),
         in_specs=[vmem, vmem, vmem] + [hbm] * 6,
         out_specs=(vmem, vmem),
@@ -564,20 +595,18 @@
             pltpu.VMEM((T, L), f32),
             pltpu.VMEM((NSP // 2, HP, 2 * T), bf16),
             pltpu.VMEM((NSP // 2, HP, 2 * T), bf16),
-            pltpu.VMEM((NSP // 2, HP, C), bf16),
-            pltpu.VMEM((NSP // 2, HP, C), bf16),
+            pltpu.VMEM((NSP // 2, 4, 64, L), bf16),
+            pltpu.VMEM((4, NSP // 2, 64, L), bf16),
             pltpu.VMEM((2, T, C), f32),
             pltpu.VMEM((T, C), f32),
-            pltpu.VMEM((4, 64, L), bf16),
-            pltpu.VMEM((4, 64, L), bf16),
             pltpu.VMEM((4, 64, L), bf16),
             pltpu.VMEM((NSP, 4, 64, L), bf16),
             pltpu.VMEM((8, T, L), f32),
             pltpu.VMEM((8, T, L), f32),
             dma((6,)), dma((16,)), dma((16,)), dma((2,)), dma((2,)), dma((16,)), dma((16,)),
-            dma((8,)), dma((8,)), dma((8,)), dma((8,)),
+            dma((8,)), dma((8,)), dma((8, 4)), dma((4, 8)),
             dma((1,)), dma((1,)), dma((1,)), dma((1,)),
-            dma((4,)), dma((4,)), dma((4,)), dma((4,)), dma((4,)), dma((4,)),
+            dma((4,)), dma((4,)), dma((4,)), dma((4,)),
             dma((16,)), dma((16,)), dma((16,)), dma((16,)), dma((16,)), dma((16,)),
         ],
         compiler_params=pltpu.CompilerParams(
@@ -588,7 +617,24 @@
         conv_weight.reshape(3, 3 * C, C), time_weight, qkv_weight, out_weight,
         cotangent.reshape(T, C),
     )
-    return updated.reshape(1, ROWS, W, C), grad.astype(f32)
+    updated, out_grad = pl.pallas_call(
+        outputs,
+        out_shape=(
+            jax.ShapeDtypeStruct((T, C), bf16),
+            jax.ShapeDtypeStruct((C, C), f32),
+        ),
+        in_specs=[hbm, hbm],
+        out_specs=(hbm, hbm),
+        scratch_shapes=[
+            pltpu.VMEM((NSP, 4, 64, L), bf16),
+            pltpu.VMEM((T, C), bf16),
+            pltpu.VMEM((C, C), f32),
+            dma((HEADS + 1,)),
+        ],
+        compiler_params=pltpu.CompilerParams(vmem_limit_bytes=63 * 2**20),
+        name="outputs",
+    )(tiles, updated)
+    return updated.reshape(1, ROWS, W, C), out_grad
 
 
 def solution(mesh):

time: 93.8 us -> 89.1 us (0.950)
  other arithmetic: 2.47 us -> 0 us
  Pallas kernels: 89.1 us -> 87.5 us
    pallas_call x1, Pallas kernels: 89.1 us -> 85.2 us  [on_device(): pl.pallas_call(kernel, out_shape=(jax.ShapeDtypeStruct((T, C), bf16), jax...]
    convert_element_type x1 -> x0, other arithmetic: 2.47 us -> none  [on_device(): return (updated.reshape(1, ROWS, W, C), grad.astype(f32))]
    pallas_call x0 -> x1, Pallas kernels: none -> 2.33 us  [on_device(): pl.pallas_call(outputs, out_shape=(jax.ShapeDtypeStruct((T, C), bf16), ja...]
where the time goes in v3:
time: 89.1 us; the launch traced here: 89 us
  Pallas kernels  87.5 us (98%)
  between operations  1.45 us (2%)
    pallas_call x1, Pallas kernels, on_device(): pl.pallas_call(kernel, out_shape=(jax.ShapeDtypeStruct((T, C), bf16), jax...  85.2 us
    pallas_call x1, Pallas kernels, on_device(): pl.pallas_call(outputs, out_shape=(jax.ShapeDtypeStruct((T, C), bf16), ja...  2.33 us

profile of v3, /device:TPU:1, one launch (start us, length us, event | category | flops | bytes accessed | tf_op | source)
XLA Modules:
  0.0 89.0 jit_solution(9275187090587767586)
XLA Ops:
  1.3 85.2 %level.1 = (bf16[256,640]{1,0:T(8,128)(2,1)}, bf16[16,4,64,128]{3,2,1,0:T(8,128)(2,1)}) custom-call(s32[1]{0:T(128)S(6)} %copy.11.ts_ref, f32[640]{0:T(1024)} %ggain_ref.1, f32[640]{0:T(1024)} %ngain_ref.1, bf16[256,640]{1,0:T(8,128)(2,1)} %bitcast.5, bf16[3,1920,640]{2,1,0:T(8,128)(2,1)} %bitcast.4, bf16[320,640]{1,0:T(8,128)(2,1)} %timew_hbm.1, ...), custom_call_target="tpu_custom_call" | custom-call | tf_op jit(solution)/shard_map/level/pallas_call | solution.py:572
  86.5 2.3 %outputs.1 = (bf16[256,640]{1,0:T(8,128)(2,1)}, f32[640,640]{1,0:T(8,128)}) custom-call(bf16[16,4,64,128]{3,2,1,0:T(8,128)(2,1)} %get-tuple-element.6.fin_hbm, bf16[256,640]{1,0:T(8,128)(2,1)} %get-tuple-element.7.upd_hbm), custom_call_target="tpu_custom_call" | custom-call | tf_op jit(solution)/shard_map/outputs/pallas_call | solution.py:620

commit v4 on v3

--- a/solution.py
+++ b/solution.py
@@ -44,11 +44,11 @@
 
 def kernel(
     ts_ref, ggain_ref, ngain_ref, feat_hbm, convw_hbm, timew_hbm, qkvw_hbm, outw_hbm, cot_hbm,
-    upd_ref, fin_out,
+    upd_out, fin_out,
     fext, convw, timew, qkvw, outw, cot, wq, wo, cols, hid, stat, xsend, x, s_buf, m_buf,
     at_send, at, g_send, g, part, other, zs, fin, z_own, m_own,
     local_sem, stat_ss, stat_rs, halo_ss, halo_rs, x_ss, x_rs, at_ss, at_rs, g_ss, g_rs,
-    cot_ss, cot_rs, part_ss, part_rs, zs_ss, zs_rs, ag_ss, ag_rs, fin_ss, fin_rs, rest_ss, rest_rs, core_ss, core_rs,
+    cot_ss, cot_rs, part_ss, part_rs, zs_ss, zs_rs, ag_ss, ag_rs, fin_ss, fin_rs, rest_ss, rest_rs, core_ss, core_rs, fin_sem,
 ):
     me = lax.axis_index("sp")
     dp = lax.axis_index("dp")
@@ -85,6 +85,12 @@
             body(i)
             return c
         lax.fori_loop(lo, hi, step, 0)
+
+    def fetch(i, src, dst):
+        c = pltpu.make_async_copy(src, dst, local_sem.at[i])
+        c.start()
+        return c
+    get_feat = fetch(0, feat_hbm, fext.at[W:W + T])
 
     barrier = pltpu.get_barrier_semaphore()
 
@@ -100,12 +106,6 @@
             pl.semaphore_signal(barrier, inc=1, device_id={"dp": x_peer(t), "sp": 2 * c + core},
                                 device_id_type=pl.DeviceIdType.MESH)
     loop(1, NSP, greet)
-
-    def fetch(i, src, dst):
-        c = pltpu.make_async_copy(src, dst, local_sem.at[i])
-        c.start()
-        return c
-    get_feat = fetch(0, feat_hbm, fext.at[W:W + T])
 
     chan = lax.broadcasted_iota(jnp.int32, (C, L), 0)
     grp = lax.broadcasted_iota(jnp.int32, (C, L), 1)
@@ -182,8 +182,6 @@
         here = slice(HP * (j // 2), HP * (j // 2) + HP)
         wo[j % 2, here] = jnp.concatenate(
             [rows, jnp.zeros((HP - HD, C), f32)], axis=0).astype(bf16)
-    at[chip] = jnp.zeros((HP, 2 * T), bf16)
-    g_send[...] = jnp.zeros(g_send.shape, bf16)
 
     loop(1, NSP, lambda t: to_sp(
         stat.at[sp_peer(t)], stat.at[sp_peer(t)], stat_ss.at[sp_peer(t)],
@@ -345,10 +343,16 @@
             device_id_type=pl.DeviceIdType.MESH)
 
     def put_g(c, rows):
-        for i in range(15):
-            a, b = i // 5, i % 5
-            g_send[c, i // 4, 16 * (i % 4):16 * (i % 4) + 16] = (
-                rows[16 * a:16 * a + 16, L * b:L * b + L])
+        low = [rows[32:HD, L * b:L * b + L] for b in range(5)] + [jnp.zeros((8, L), f32)]
+        for i in range(12):
+            if i < 10:
+                tile = rows[16 * (i // 5):16 * (i // 5) + 16, L * (i % 5):L * (i % 5) + L]
+            else:
+                tile = jnp.concatenate(low[2 * i - 20:2 * i - 18], axis=0)
+            g_send[c, i // 3, 16 * (i % 3):16 * (i % 3) + 16] = tile.astype(bf16)
+        spare = jnp.concatenate(low[4:], axis=0).astype(bf16)
+        for k in range(4):
+            g_send[c, k, 48:64] = spare
 
     def i32(v):
         return jnp.int32(v)
@@ -369,39 +373,30 @@
     swap_cot.wait_recv()
     cots = cot.reshape(2 * T, C)
 
-    def grads(p, live):
-        c = lax.select(live, source(p), chip)
-
-        @pl.when(live)
-        def _():
-            recv_at(c).wait_recv()
-
-        put_g(c, jnp.dot(at[c], cots[...], preferred_element_type=f32).astype(bf16))
+    def grads(p):
+        c = source(p)
+        recv_at(c).wait_recv()
+        put_g(c, jnp.dot(at[c], cots[...], preferred_element_type=f32))
 
         def start():
-            @pl.when(live)
-            def _():
-                for k in range(4):
-                    send_g(c, k).start()
+            for k in range(4):
+                send_g(c, k).start()
         return start
 
     begin(query(2 * target(i32(0))), "all")
 
     def cross_pair(u, last):
-        start = grads(i32(0), jnp.bool_(True)) if last else None
         now, later = target(u), target(u + 1)
         acc, _ = attend("all", 0, (query(2 * now + 1), "all"))
         at_send[now, :, 0:T] = finish(acc)
         acc, _ = attend("all", 1, (query(2 * later), "other" if last else "all"))
         at_send[now, :, T:2 * T] = finish(acc)
         send_at(now).start()
-        if last:
-            start()
     loop(0, 3, lambda u: cross_pair(u, False))
     cross_pair(i32(3), True)
 
     def side_pair(u, last):
-        start = grads(lax.select(u == 3, 3, u + 1), u != 2)
+        start = grads(u)
         now, later = target(4 + u), target(4 + lax.rem(u + 1, 4))
         acc, _ = attend("other", 0, (query(2 * now + 1), "other"), before=2 * u)
         at_send[now, :, 0:T] = finish(acc)
@@ -419,7 +414,7 @@
     for c in last:
         recv_at(c).wait_recv()
     block = jnp.concatenate([at[c] for c in last] + [at[chip]], axis=0)
-    final = jnp.dot(block, cots[...], preferred_element_type=f32).astype(bf16)
+    final = jnp.dot(block, cots[...], preferred_element_type=f32)
     for i, c in enumerate(last):
         put_g(c, final[i * HP:(i + 1) * HP])
         for k in range(4):
@@ -453,21 +448,47 @@
     swap_part = to_sp(part.at[1 - core], other, part_ss.at[0], part_rs.at[0], sibling)
     swap_part.start()
 
+    @pl.when(me > 0)
+    def _():
+        up.wait_send()
+
+    @pl.when(me < NSP - 1)
+    def _():
+        down.wait_send()
+
+    def drain(t):
+        j = sp_peer(t)
+        to_sp(stat.at[me], stat.at[me], stat_ss.at[j], stat_rs.at[me], j).wait_send()
+        send_x(j).wait_send()
+    loop(1, NSP, drain)
+
+    def drain_pair(t):
+        c = lax.rem(chip + t, NSP // 2)
+        send_at(c).wait_send()
+        for k in range(4):
+            send_g(c, k).wait_send()
+    loop(1, NSP // 2, drain_pair)
+    swap_cot.wait_send()
+    for t in range(1, 4):
+        send_g(chip, lax.rem(xi + t, 4)).wait_send()
+
     for t in (1, 3, 2):
         k = lax.rem(zh + t, 4)
         to_dp(zs.at[k], zs.at[k], zs_ss.at[t], zs_rs.at[k], zh_peer(t)).wait_recv()
-    fin[me, 0] = jnp.sum(zs[...].astype(f32), axis=0).astype(bf16)
+    fin[me, 0:64] = jnp.sum(zs[...].astype(f32), axis=0).astype(bf16)
 
     def send_ag(t):
-        return to_dp(fin.at[me, 0], fin.at[me, 4 - t], ag_ss.at[t], ag_rs.at[4 - t], x_peer(t))
+        return to_dp(fin.at[me, pl.ds(0, 48)], fin.at[me, pl.ds(64 + 48 * (3 - t), 48)],
+                     ag_ss.at[t], ag_rs.at[4 - t], x_peer(t))
 
     def send_own(u):
         j = lax.rem(me + 2 * u, NSP)
-        return to_sp(fin.at[me, 0], fin.at[me, 0], fin_ss.at[j], fin_rs.at[me], j)
+        return to_sp(fin.at[me, pl.ds(0, 64)], fin.at[me, pl.ds(0, 64)], fin_ss.at[j],
+                     fin_rs.at[me], j)
 
     def send_rest(u):
         j = lax.rem(me + 2 * u, NSP)
-        return to_sp(fin.at[me, pl.ds(1, 3)], fin.at[me, pl.ds(1, 3)], rest_ss.at[j],
+        return to_sp(fin.at[me, pl.ds(64, 144)], fin.at[me, pl.ds(64, 144)], rest_ss.at[j],
                      rest_rs.at[me], j)
     def pass_on(j):
         return to_sp(fin.at[j], fin.at[j], core_ss.at[j], core_rs.at[j], sibling)
@@ -475,61 +496,45 @@
         send_ag(t).start()
     loop(1, NSP // 2, lambda u: send_own(u).start())
     swap_part.wait_recv()
-    upd_ref[...] = (hid[...].astype(f32) + part[core] + other[...]).astype(bf16)
+    hid[...] = (hid[...].astype(f32) + part[core] + other[...]).astype(bf16)
+    put_upd = pltpu.make_async_copy(hid, upd_out, local_sem.at[0])
+    put_upd.start()
 
     for k in (1, 3, 2):
-        to_dp(fin.at[me, k], fin.at[me, k], ag_ss.at[k], ag_rs.at[k], x_peer(k)).wait_recv()
+        quarter = fin.at[me, pl.ds(64 + 48 * (k - 1), 48)]
+        to_dp(quarter, quarter, ag_ss.at[k], ag_rs.at[k], x_peer(k)).wait_recv()
     loop(1, NSP // 2, lambda u: send_rest(u).start())
     pass_on(me).start()
 
+    def put_fin(j):
+        return pltpu.make_async_copy(fin.at[j], fin_out.at[j], fin_sem.at[j])
+    put_fin(me).start()
+    swap_part.wait_send()
+    for t in range(1, 4):
+        send_zs(t).wait_send()
+        send_ag(t).wait_send()
+    loop(1, NSP // 2, lambda u: send_own(u).wait_send())
+
     def relay(u):
         j = lax.rem(me + NSP - 2 * u, NSP)
-        to_sp(fin.at[j, 0], fin.at[j, 0], fin_ss.at[j], fin_rs.at[j], j).wait_recv()
-        to_sp(fin.at[j, pl.ds(1, 3)], fin.at[j, pl.ds(1, 3)], rest_ss.at[j], rest_rs.at[j],
-              j).wait_recv()
+        own, rest = fin.at[j, pl.ds(0, 64)], fin.at[j, pl.ds(64, 144)]
+        to_sp(own, own, fin_ss.at[j], fin_rs.at[j], j).wait_recv()
+        to_sp(rest, rest, rest_ss.at[j], rest_rs.at[j], j).wait_recv()
         pass_on(j).start()
+        put_fin(j).start()
     loop(1, NSP // 2, relay)
+    loop(1, NSP // 2, lambda u: send_rest(u).wait_send())
 
     def recv_core(u):
         j = lax.rem(sibling + NSP - 2 * u, NSP)
         to_sp(fin.at[j], fin.at[j], core_ss.at[j], core_rs.at[j], sibling).wait_recv()
+        put_fin(j).start()
     loop(0, NSP // 2, recv_core)
 
-    fin_out[...] = fin[...]
-
-    @pl.when(me > 0)
-    def _():
-        up.wait_send()
-
-    @pl.when(me < NSP - 1)
-    def _():
-        down.wait_send()
-
-    def drain(t):
-        j = sp_peer(t)
-        to_sp(stat.at[me], stat.at[me], stat_ss.at[j], stat_rs.at[me], j).wait_send()
-        send_x(j).wait_send()
-    loop(1, NSP, drain)
-
-    def drain_pair(t):
-        c = lax.rem(chip + t, NSP // 2)
-        send_at(c).wait_send()
-        for k in range(4):
-            send_g(c, k).wait_send()
-    loop(1, NSP // 2, drain_pair)
-    swap_cot.wait_send()
-    swap_part.wait_send()
-    for t in range(1, 4):
-        send_g(chip, lax.rem(xi + t, 4)).wait_send()
-        send_zs(t).wait_send()
-        send_ag(t).wait_send()
-
-    def drain_fin(u):
-        send_own(u).wait_send()
-        send_rest(u).wait_send()
-        pass_on(lax.rem(me + NSP - 2 * u, NSP)).wait_send()
-    loop(1, NSP // 2, drain_fin)
+    loop(1, NSP // 2, lambda u: pass_on(lax.rem(me + NSP - 2 * u, NSP)).wait_send())
     pass_on(me).wait_send()
+    put_upd.wait()
+    loop(0, NSP, lambda j: put_fin(j).wait())
 
 
 def outputs(fin_hbm, upd_hbm, upd_out, grad_out, fin, upd, grad, sem):
@@ -543,16 +548,17 @@
     for j in range(0, HEADS, 2):
         get(j).start()
     take.start()
-    quarter = [lax.rem(k + 4 - xi, 4) for k in range(4)]
+    turn = [lax.rem(k + 4 - xi, 4) for k in range(4)]
+    start = [pl.multiple_of(lax.select(r == 0, 0, 16 + 48 * r), 16) for r in turn]
 
     def head_rows(j):
-        tiles = [fin[j, quarter[i // 4], 16 * (i % 4):16 * (i % 4) + 16] for i in range(15)]
-        return jnp.concatenate(
-            [jnp.concatenate(tiles[5 * a:5 * a + 5], axis=1) for a in range(3)], axis=0)
+        tiles = [fin[j, pl.ds(start[i // 3] + 16 * (i % 3), 16)].astype(f32) for i in range(12)]
+        spare = fin[j, 48:64].astype(f32)
+        low = [tiles[10][:8], tiles[10][8:], tiles[11][:8], tiles[11][8:], spare[:8]]
+        return [jnp.concatenate(row, axis=1) for row in (tiles[:5], tiles[5:10], low)]
     for j in range(0, HEADS, 2):
         get(j).wait()
-        two = jnp.concatenate(
-            [head_rows(j).astype(f32)[:HD], head_rows(j + 1).astype(f32)[:HD]], axis=0)
+        two = jnp.concatenate(head_rows(j) + head_rows(j + 1), axis=0)
         here = slice(HD * j, HD * j + 2 * HD)
         grad[here] = two
         pltpu.make_async_copy(grad.at[here], grad_out.at[here], sem.at[j // 2]).start()
@@ -573,10 +579,10 @@
         kernel,
         out_shape=(
             jax.ShapeDtypeStruct((T, C), bf16),
-            jax.ShapeDtypeStruct((NSP, 4, 64, L), bf16),
+            jax.ShapeDtypeStruct((NSP, 13 * 16, L), bf16),
         ),
         in_specs=[vmem, vmem, vmem] + [hbm] * 6,
-        out_specs=(vmem, vmem),
+        out_specs=(hbm, hbm),
         scratch_shapes=[
             pltpu.VMEM((4 * W, C), bf16),
             pltpu.VMEM((3, 3 * C, C), bf16),
@@ -600,14 +606,14 @@
             pltpu.VMEM((2, T, C), f32),
             pltpu.VMEM((T, C), f32),
             pltpu.VMEM((4, 64, L), bf16),
-            pltpu.VMEM((NSP, 4, 64, L), bf16),
+            pltpu.VMEM((NSP, 13 * 16, L), bf16),
             pltpu.VMEM((8, T, L), f32),
             pltpu.VMEM((8, T, L), f32),
             dma((6,)), dma((16,)), dma((16,)), dma((2,)), dma((2,)), dma((16,)), dma((16,)),
             dma((8,)), dma((8,)), dma((8, 4)), dma((4, 8)),
             dma((1,)), dma((1,)), dma((1,)), dma((1,)),
             dma((4,)), dma((4,)), dma((4,)), dma((4,)),
-            dma((16,)), dma((16,)), dma((16,)), dma((16,)), dma((16,)), dma((16,)),
+            dma((16,)), dma((16,)), dma((16,)), dma((16,)), dma((16,)), dma((16,)), dma((16,)),
         ],
         compiler_params=pltpu.CompilerParams(
             collective_id=0, has_side_effects=True, vmem_limit_bytes=60 * 2**20),
@@ -626,7 +632,7 @@
         in_specs=[hbm, hbm],
         out_specs=(hbm, hbm),
         scratch_shapes=[
-            pltpu.VMEM((NSP, 4, 64, L), bf16),
+            pltpu.VMEM((NSP, 13 * 16, L), bf16),
             pltpu.VMEM((T, C), bf16),
             pltpu.VMEM((C, C), f32),
             dma((HEADS + 1,)),

time: 89.1 us -> 87.2 us (0.979)
  Pallas kernels: 87.5 us -> 85.6 us
    pallas_call x1, Pallas kernels: 85.2 us -> 83.3 us  [on_device(): pl.pallas_call(kernel, out_shape=(jax.ShapeDtypeStruct((T, C), bf16), jax...]
where the time goes in v4:
time: 87.2 us; the launch traced here: 87 us
  Pallas kernels  85.6 us (98%)
  between operations  1.45 us (2%)
    pallas_call x1, Pallas kernels, on_device(): pl.pallas_call(kernel, out_shape=(jax.ShapeDtypeStruct((T, C), bf16), jax...  83.3 us
    pallas_call x1, Pallas kernels, on_device(): pl.pallas_call(outputs, out_shape=(jax.ShapeDtypeStruct((T, C), bf16), ja...  2.33 us

profile of v4, /device:TPU:1, one launch (start us, length us, event | category | flops | bytes accessed | tf_op | source)
XLA Modules:
  0.0 87.0 jit_solution(7131226109133852315)
XLA Ops:
  1.3 83.3 %level.1 = (bf16[256,640]{1,0:T(8,128)(2,1)}, bf16[16,208,128]{2,1,0:T(8,128)(2,1)}) custom-call(s32[1]{0:T(128)S(6)} %copy.11.ts_ref, f32[640]{0:T(1024)} %ggain_ref.1, f32[640]{0:T(1024)} %ngain_ref.1, bf16[256,640]{1,0:T(8,128)(2,1)} %bitcast.5, bf16[3,1920,640]{2,1,0:T(8,128)(2,1)} %bitcast.4, bf16[320,640]{1,0:T(8,128)(2,1)} %timew_hbm.1, ...), custom_call_target="tpu_custom_call" | custom-call | tf_op jit(solution)/shard_map/level/pallas_call | solution.py:578
  84.5 2.3 %outputs.1 = (bf16[256,640]{1,0:T(8,128)(2,1)}, f32[640,640]{1,0:T(8,128)}) custom-call(bf16[16,208,128]{2,1,0:T(8,128)(2,1)} %get-tuple-element.6.fin_hbm, bf16[256,640]{1,0:T(8,128)(2,1)} %get-tuple-element.7.upd_hbm), custom_call_target="tpu_custom_call" | custom-call | tf_op jit(solution)/shard_map/outputs/pallas_call | solution.py:626

commit v5 on v4

--- a/solution.py
+++ b/solution.py
@@ -172,16 +172,6 @@
             piece = jnp.where(lane < 3 * HD, piece, 0.0).astype(bf16)
             wq[j // 2, here, (j % 2) * L:(j % 2) * L + L] = piece
     loop(0, C // L, regroup)
-    get_outw.wait()
-    for j in range(HEADS):
-        if (HD * j) % 16 == 0:
-            rows = outw[HD * j:HD * j + HP] if j < HEADS - 1 else outw[HD * j:HD * j + HD]
-            rows = rows.astype(f32)[:HD]
-        else:
-            rows = outw[HD * j - 8:HD * j + HD].astype(f32)[8:]
-        here = slice(HP * (j // 2), HP * (j // 2) + HP)
-        wo[j % 2, here] = jnp.concatenate(
-            [rows, jnp.zeros((HP - HD, C), f32)], axis=0).astype(bf16)
 
     loop(1, NSP, lambda t: to_sp(
         stat.at[sp_peer(t)], stat.at[sp_peer(t)], stat_ss.at[sp_peer(t)],
@@ -263,6 +253,17 @@
 
     def recv_x(j):
         to_sp(x.at[j], x.at[j], x_ss.at[j], x_rs.at[j], j).wait_recv()
+    get_outw.wait()
+    for j in range(HEADS):
+        if (HD * j) % 16 == 0:
+            rows = outw[HD * j:HD * j + HP] if j < HEADS - 1 else outw[HD * j:HD * j + HD]
+            rows = rows.astype(f32)[:HD]
+        else:
+            rows = outw[HD * j - 8:HD * j + HD].astype(f32)[8:]
+        here = slice(HP * (j // 2), HP * (j // 2) + HP)
+        wo[j % 2, here] = jnp.concatenate(
+            [rows, jnp.zeros((HP - HD, C), f32)], axis=0).astype(bf16)
+
     for dy in range(4):
         for dc in range(2):
             if dy or dc:
@@ -359,17 +360,24 @@
 
     begin(query(2 * target(i32(4))), "own")
 
-    def own_pair(u):
-        now, later = target(4 + u), target(4 + lax.rem(u + 1, 4))
+    def own_pair(u, last):
+        now, later = target(4 + u), target(5 + u)
         for k in range(2):
-            acc, m = attend("own", k, (query(2 * now + 1 if k == 0 else 2 * later), "own"))
+            if k == 0:
+                nxt = (query(2 * now + 1), "own")
+            elif not last:
+                nxt = (query(2 * later), "own")
+            else:
+                for dy in range(4):
+                    for dc in range(2):
+                        recv_x(slab(dy, 1, dc))
+                nxt = (query(2 * target(i32(0))), "all")
+            acc, m = attend("own", k, nxt)
             z_own[2 * u + k] = acc
             m_own[2 * u + k] = jnp.broadcast_to(m, (T, L))
-    loop(0, 4, own_pair)
-
-    for dy in range(4):
-        for dc in range(2):
-            recv_x(slab(dy, 1, dc))
+    loop(0, 3, lambda u: own_pair(u, False))
+    own_pair(i32(3), True)
+
     swap_cot.wait_recv()
     cots = cot.reshape(2 * T, C)
 
@@ -382,8 +390,6 @@
             for k in range(4):
                 send_g(c, k).start()
         return start
-
-    begin(query(2 * target(i32(0))), "all")
 
     def cross_pair(u, last):
         now, later = target(u), target(u + 1)
@@ -411,17 +417,18 @@
 
     at[chip] = at_send[chip]
     last = [source(i32(p)) for p in (4, 5, 6)]
-    for c in last:
+    for c in last[:2]:
         recv_at(c).wait_recv()
-    block = jnp.concatenate([at[c] for c in last] + [at[chip]], axis=0)
+    block = jnp.concatenate([at[last[0]], at[last[1]], at[chip]], axis=0)
     final = jnp.dot(block, cots[...], preferred_element_type=f32)
-    for i, c in enumerate(last):
+    for i, c in enumerate(last[:2]):
         put_g(c, final[i * HP:(i + 1) * HP])
         for k in range(4):
             send_g(c, k).start()
-    put_g(chip, final[3 * HP:])
+    put_g(chip, final[2 * HP:])
     for t in range(1, 4):
         send_g(chip, lax.rem(xi + t, 4)).start()
+    grads(i32(6))()
     g[xi, chip] = g_send[chip, xi]
 
     def recv_g(t):

time: 87.2 us -> 85.7 us (0.983)
  Pallas kernels: 85.6 us -> 84.1 us
    pallas_call x1, Pallas kernels: 83.3 us -> 81.8 us  [on_device(): pl.pallas_call(kernel, out_shape=(jax.ShapeDtypeStruct((T, C), bf16), jax...]
where the time goes in v5:
time: 85.7 us; the launch traced here: 85.6 us
  Pallas kernels  84.1 us (98%)
  between operations  1.45 us (2%)
    pallas_call x1, Pallas kernels, on_device(): pl.pallas_call(kernel, out_shape=(jax.ShapeDtypeStruct((T, C), bf16), jax...  81.8 us
    pallas_call x1, Pallas kernels, on_device(): pl.pallas_call(outputs, out_shape=(jax.ShapeDtypeStruct((T, C), bf16), ja...  2.33 us

profile of v5, /device:TPU:1, one launch (start us, length us, event | category | flops | bytes accessed | tf_op | source)
XLA Modules:
  0.0 85.6 jit_solution(17126459537731825715)
XLA Ops:
  1.3 81.8 %level.1 = (bf16[256,640]{1,0:T(8,128)(2,1)}, bf16[16,208,128]{2,1,0:T(8,128)(2,1)}) custom-call(s32[1]{0:T(128)S(6)} %copy.11.ts_ref, f32[640]{0:T(1024)} %ggain_ref.1, f32[640]{0:T(1024)} %ngain_ref.1, bf16[256,640]{1,0:T(8,128)(2,1)} %bitcast.5, bf16[3,1920,640]{2,1,0:T(8,128)(2,1)} %bitcast.4, bf16[320,640]{1,0:T(8,128)(2,1)} %timew_hbm.1, ...), custom_call_target="tpu_custom_call" | custom-call | tf_op jit(solution)/shard_map/level/pallas_call | solution.py:585
  83.1 2.3 %outputs.1 = (bf16[256,640]{1,0:T(8,128)(2,1)}, f32[640,640]{1,0:T(8,128)}) custom-call(bf16[16,208,128]{2,1,0:T(8,128)(2,1)} %get-tuple-element.6.fin_hbm, bf16[256,640]{1,0:T(8,128)(2,1)} %get-tuple-element.7.upd_hbm), custom_call_target="tpu_custom_call" | custom-call | tf_op jit(solution)/shard_map/outputs/pallas_call | solution.py:633
